TPU v7x, 128 devices: a whole 4x4x4 slice. The times are simulated.
128 devices in a mesh: group: 8 (over y, core), lend: 16 (over x, z).
Axes of the slice: x: 4, y: 4, z: 4, core: 2. Of those that a mesh axis runs over, the one named last changes fastest.
Arguments:
- tokens: bfloat16 [2, 64, 8192], replicated, may hold values from -6 to 6
- query_weight: bfloat16 [8192, 8192], P('group', 'lend'), may hold values from -0.0625 to 0.0625
- kv_weight: bfloat16 [8192, 2048], P(('group', 'lend')), may hold values from -0.0625 to 0.0625
- pages: bfloat16 [4096, 2, 128, 1024], P(('group', 'lend')), may hold values from -300 to 300
- slot_request: int32 [4096], P(('group', 'lend')), may hold values from 0 to 63
- slot_len: int32 [4096], P(('group', 'lend')), may hold values from 0 to 128, as said below
Outputs:
- attended: bfloat16 [2, 64, 8192], P(None, 'group', 'lend')
Inputs may be any that keep to these rules, and one draw needn't show every extreme that they name: `slot_len`: slot lengths are positive exactly in the first slots of each device, at least 16 of them; some device has all 32 slots in use.
All inputs are finite; a program needn't handle non-finite values.
Results may differ from a plain program's by a relative error of at most 0.012.
The roundings to bfloat16 on the way count: a program that leaves them out, or rounds other values in their place, can miss the bound.
Values may be sent and summed in bfloat16 or wider, within the bound.
A program may use at most 128 MiB of HBM per device.

v0:
```python
import jax
import jax.numpy as jnp
from jax import lax
from jax.sharding import PartitionSpec as P

HQ = 64
KVH = 8
HD = 128
PAGE = 128


page_block = 2


def combine_parts(first, second):
    maxima = jnp.maximum(first[0], second[0])
    left = jnp.exp(first[0] - maxima)
    right = jnp.exp(second[0] - maxima)
    totals = first[1] * left + second[1] * right
    weighted = first[2] * left[..., None] + second[2] * right[..., None]
    return (maxima, totals, weighted)


def fold_parts(maxima, totals, weighted):
    highest = jnp.max(maxima, axis=0)
    factor = jnp.exp(maxima - highest)
    return (
        highest,
        jnp.sum(totals * factor, axis=0),
        jnp.sum(weighted * factor[..., None], axis=0),
    )


def page_partial(queries, page_rows, owners, lengths, page_ok, requests):
    count = page_rows.shape[0]
    key_rows = page_rows[:, 0].reshape(count, PAGE, KVH, HD)
    value_rows = page_rows[:, 1].reshape(count, PAGE, KVH, HD).astype(jnp.float32)
    chosen = jnp.take(queries, owners, axis=0)
    scores = jnp.einsum(
        "pkgd,ptkd->pkgt", chosen, key_rows, preferred_element_type=jnp.float32
    ) / jnp.sqrt(jnp.float32(HD))
    positions = jnp.arange(PAGE, dtype=jnp.int32)
    valid = page_ok[:, None, None, None] & (
        positions[None, None, None, :] < lengths[:, None, None, None]
    )
    owned = (owners[:, None] == jnp.arange(requests, dtype=jnp.int32)[None, :]) & page_ok[:, None]
    page_max = jnp.max(jnp.where(valid, scores, -1e30), axis=3)
    maxima = jnp.max(jnp.where(owned[:, :, None, None], page_max[:, None], -1e30), axis=0)
    anchor = jnp.take(maxima, owners, axis=0)
    weights = jnp.where(valid, jnp.exp(scores - anchor[..., None]), 0.0)
    owned_float = owned.astype(jnp.float32)
    totals = jnp.einsum(
        "pr,pkg->rkg", owned_float, jnp.sum(weights, axis=3), precision=lax.Precision.HIGHEST
    )
    per_page = jnp.einsum("pkgt,ptkd->pkgd", weights, value_rows, precision=lax.Precision.HIGHEST)
    weighted = jnp.einsum("pr,pkgd->rkgd", owned_float, per_page, precision=lax.Precision.HIGHEST)
    return (maxima, totals, weighted)


def attend_range(carried, queries, page_rows, owners, lengths, lower, upper):
    requests = queries.shape[0]

    def visit(block_index, current):
        start = block_index * page_block
        block_rows = lax.dynamic_slice_in_dim(page_rows, start, page_block, 0)
        block_owner = lax.dynamic_slice_in_dim(owners, start, page_block, 0)
        block_len = lax.dynamic_slice_in_dim(lengths, start, page_block, 0)
        page_index = start + jnp.arange(page_block, dtype=jnp.int32)
        page_ok = (page_index >= lower) & (page_index < upper)
        part = page_partial(queries, block_rows, block_owner, block_len, page_ok, requests)
        return combine_parts(current, part)

    first_block = lower // page_block
    last_block = (upper + page_block - 1) // page_block
    return lax.fori_loop(first_block, last_block, visit, carried)


def fresh_partial(queries, fresh, owned):
    count = fresh.shape[0]
    requests = fresh.shape[1]
    key_rows = fresh[:, :, : KVH * HD].reshape(count, requests, KVH, HD)
    value_rows = fresh[:, :, KVH * HD :].reshape(count, requests, KVH, HD).astype(jnp.float32)
    scores = jnp.einsum(
        "rkgd,trkd->rkgt", queries, key_rows, preferred_element_type=jnp.float32
    ) / jnp.sqrt(jnp.float32(HD))
    maxima = jnp.where(owned[:, None, None], jnp.max(scores, axis=3), -1e30)
    weights = jnp.where(owned[:, None, None, None], jnp.exp(scores - maxima[..., None]), 0.0)
    weighted = jnp.einsum("rkgt,trkd->rkgd", weights, value_rows, precision=lax.Precision.HIGHEST)
    return (maxima, jnp.sum(weights, axis=3), weighted)


def per_device(tokens, query_weight, kv_weight, pages, slot_request, slot_len):
    n_group = lax.axis_size("group")
    n_lend = lax.axis_size("lend")
    devices = n_group * n_lend
    flat_index = lax.axis_index("group") * n_lend + lax.axis_index("lend")
    steps_here = tokens.shape[0]
    requests = tokens.shape[1]
    grouped = HQ // KVH
    heads_local = HQ // n_lend
    req_local = requests // n_group
    query_rows = query_weight.shape[0]
    token_part = lax.dynamic_slice_in_dim(
        tokens, lax.axis_index("group") * query_rows, query_rows, 2
    )
    query_part = jnp.einsum(
        "srd,de->sre", token_part, query_weight, preferred_element_type=jnp.float32
    )
    query_sum = lax.psum(query_part, "group").astype(jnp.bfloat16)
    all_queries = lax.all_gather(query_sum, "lend", axis=2, tiled=True)
    kv_rows = kv_weight.shape[0]
    token_slice = lax.dynamic_slice_in_dim(tokens, flat_index * kv_rows, kv_rows, 2)
    fresh_part = jnp.einsum(
        "srd,de->sre", token_slice, kv_weight, preferred_element_type=jnp.float32
    )
    fresh = lax.psum(fresh_part, ("group", "lend")).astype(jnp.bfloat16)
    live = jnp.sum((slot_len > 0).astype(jnp.int32))
    ranges = (pages, slot_request, slot_len, 0, live)
    owned = jnp.arange(requests, dtype=jnp.int32) % devices == flat_index
    results = []
    for step_index in range(steps_here):
        queries = all_queries[step_index].reshape(requests, KVH, grouped, HD)
        carried = (
            jnp.full((requests, KVH, grouped), -1e30, jnp.float32),
            jnp.zeros((requests, KVH, grouped), jnp.float32),
            jnp.zeros((requests, KVH, grouped, HD), jnp.float32),
        )
        page_rows, owners, lengths, lower, upper = ranges
        carried = attend_range(carried, queries, page_rows, owners, lengths, lower, upper)
        carried = combine_parts(carried, fresh_partial(queries, fresh[: step_index + 1], owned))
        maxima = carried[0].reshape(requests, HQ)
        totals = carried[1].reshape(requests, HQ)
        weighted = carried[2].reshape(requests, HQ, HD)
        maxima = (
            maxima.reshape(n_group, req_local, n_lend, heads_local)
            .transpose(0, 2, 1, 3)
            .reshape(1, devices, req_local, heads_local)
        )
        totals = (
            totals.reshape(n_group, req_local, n_lend, heads_local)
            .transpose(0, 2, 1, 3)
            .reshape(1, devices, req_local, heads_local)
        )
        weighted = (
            weighted.reshape(n_group, req_local, n_lend, heads_local, HD)
            .transpose(0, 2, 1, 3, 4)
            .reshape(1, devices, req_local, heads_local, HD)
        )
        arrived = (
            lax.all_to_all(maxima, ("group", "lend"), split_axis=1, concat_axis=0, tiled=True),
            lax.all_to_all(totals, ("group", "lend"), split_axis=1, concat_axis=0, tiled=True),
            lax.all_to_all(weighted, ("group", "lend"), split_axis=1, concat_axis=0, tiled=True),
        )
        merged = fold_parts(arrived[0], arrived[1], arrived[2])
        final_totals = merged[1].reshape(req_local, heads_local)
        final_weighted = merged[2].reshape(req_local, heads_local, HD)
        output = final_weighted / final_totals[..., None]
        results.append(output.astype(jnp.bfloat16).reshape(req_local, heads_local * HD))
    return jnp.stack(results)


def solution(mesh):
    return jax.shard_map(
        per_device,
        mesh=mesh,
        in_specs=(
            P(),
            P("group", "lend"),
            P(("group", "lend"), None),
            P(("group", "lend"), None, None, None),
            P(("group", "lend")),
            P(("group", "lend")),
        ),
        out_specs=P(None, "group", "lend"),
        check_vma=False,
    )
```

profile of v0, /device:TPU:1, one launch (start us, length us, event | category | flops | bytes accessed | tf_op | source)
XLA Modules:
  0.0 621.8 jit_solution(1300421286110654679)
XLA Ops:
  9.7 27.0 %all-reduce.2 = bf16[2,64,512]{2,1,0:T(8,128)(2,1)} all-reduce(f32[2,64,512]{2,1,0:T(8,128)S(1)} %fusion.33), channel_id=1, replica_groups=mesh['group'=8,'lend'=16] {'group'}, use_global_device_ids=true, to_apply=%region_1.0 | all-reduce | flops 65536 | bytes 393216 | tf_op jit(solution)/shard_map/psum | solution.py:109
  38.1 21.3 %copy.184 = bf16[32,2,128,1024]{2,3,0,1:T(8,128)(2,1)} copy(bf16[32,2,128,1024]{3,2,1,0:T(8,128)(2,1)} %param.17) | data formatting | bytes 33554432 | tf_op jit(solution)/shard_map/while | solution.py:75
  59.7 75.7 %all-reduce.3 = bf16[2,64,2048]{2,1,0:T(8,128)(2,1)S(1)} all-reduce(f32[2,64,2048]{2,1,0:T(8,128)S(1)} %fusion.43), channel_id=1, replica_groups=mesh['group'=8,'lend'=16] {'group','lend'}, use_global_device_ids=true, to_apply=%region_7.10 | all-reduce | flops 262144 | bytes 1572864 | tf_op jit(solution)/shard_map/psum | solution.py:116
  137.8 2.7 slice_bitcast_fusion.1
  142.1 122.0 %while.28 = (s32[]{:T(128)}, f32[64,8,8]{0,2,1:T(8,128)S(1)}, f32[64,8,8]{0,2,1:T(8,128)S(1)}, f32[64,8,8,128]{3,0,2,1:T(8,128)S(1)}, s32[]{:T(128)}, /*index=5*...) while((s32[]{:T(128)}, f32[64,8,8]{0,2,1:T(8,128)S(1)}, ...), condition=%wide.region_6.9_spmd, body=%wide.region_2.8_spmd.sunk | while | flops 43800224 | bytes 8039235 | solution.py:75
  167.2 2.6 multiply_add_fusion.7
  272.2 32.9 %all-to-all-start.1 = ((f32[1,128,8,4]{2,3,0,1:T(4,128)}), f32[1,128,8,4]{2,3,0,1:T(4,128)S(1)}, u32[]{:S(2)}, u32[]{:S(2)}) async-start(f32[1,128,8,4]{2,3,0,1:T(4,128)} %bitcast.19), calls=%async_computation.1 | async-start | bytes 524288 | tf_op jit(solution)/shard_map/all_to_all | solution.py:150
  307.5 146.0 %while.29 = (s32[]{:T(128)}, f32[64,8,8]{0,2,1:T(8,128)S(1)}, f32[64,8,8]{0,2,1:T(8,128)S(1)}, f32[64,8,8,128]{3,0,2,1:T(8,128)}, s32[]{:T(128)}, /*index=5*/s32...) while((s32[]{:T(128)}, f32[64,8,8]{0,2,1:T(8,128)S(1)}, ...), condition=%wide.region_15.18_spmd, body=%wide.region_11.17_spmd.sunk | while | flops 43800224 | bytes 8039235 | solution.py:75
  313.8 4.5 multiply_add_fusion.8
  325.0 4.5 multiply_add_fusion.8
  336.3 4.5 multiply_add_fusion.8
  347.5 4.5 multiply_add_fusion.8
  358.7 4.5 multiply_add_fusion.8
  369.9 4.5 multiply_add_fusion.8
  381.1 4.5 multiply_add_fusion.8
  392.4 4.5 multiply_add_fusion.8
  403.6 4.5 multiply_add_fusion.8
  414.8 4.5 multiply_add_fusion.8
  426.0 4.5 multiply_add_fusion.8
  437.2 4.5 multiply_add_fusion.8
  448.5 4.5 multiply_add_fusion.8
  456.8 43.4 %all-to-all-start.2 = ((f32[1,128,8,4]{2,3,0,1:T(4,128)}), f32[1,128,8,4]{2,3,0,1:T(4,128)S(1)}, u32[]{:S(2)}, u32[]{:S(2)}) async-start(f32[1,128,8,4]{2,3,0,1:T(4,128)} %bitcast.22), calls=%async_computation.2 | async-start | bytes 524288 | tf_op jit(solution)/shard_map/all_to_all | solution.py:151
  501.8 9.3 %all-to-all-done.2 = f32[1,128,8,4]{2,3,0,1:T(4,128)S(1)} async-done(((f32[1,128,8,4]{2,3,0,1:T(4,128)}), f32[1,128,8,4]{2,3,0,1:T(4,128)S(1)}, u32[]{:S(2)}, u32[]{:S(2)}) %all-to-all-start.2) | async-done | bytes 16416 | tf_op jit(solution)/shard_map/all_to_all | solution.py:151
  511.1 4.6 all-to-all-start.4
  516.7 9.9 %all-to-all-done.4 = f32[1,128,8,4]{2,3,0,1:T(4,128)S(1)} async-done(((f32[1,128,8,4]{2,3,0,1:T(4,128)}), f32[1,128,8,4]{2,3,0,1:T(4,128)S(1)}, u32[]{:S(2)}, u32[]{:S(2)}) %all-to-all-start.4) | async-done | bytes 16416 | tf_op jit(solution)/shard_map/all_to_all | solution.py:150
  526.6 4.6 all-to-all-start.5
  534.7 7.3 %all-to-all-done.5 = f32[1,128,8,4]{2,3,0,1:T(4,128)S(1)} async-done(((f32[1,128,8,4]{2,3,0,1:T(4,128)}), f32[1,128,8,4]{2,3,0,1:T(4,128)S(1)}, u32[]{:S(2)}, u32[]{:S(2)}) %all-to-all-start.5) | async-done | bytes 16416 | tf_op jit(solution)/shard_map/all_to_all | solution.py:151
  542.0 5.7 all-to-all-start
  549.6 5.3 fusion.32
  557.4 19.8 %all-to-all-done = f32[1,128,8,4,128]{4,2,3,0,1:T(8,128)} async-done(((f32[1,128,8,4,128]{4,2,3,0,1:T(8,128)}), f32[1,128,8,4,128]{4,2,3,0,1:T(8,128)}, u32[]{:S(2)}, u32[]{:S(2)}) %all-to-all-start) | async-done | bytes 2097184 | tf_op jit(solution)/shard_map/all_to_all | solution.py:152
  577.2 5.6 all-to-all-start.3
  585.8 26.5 %all-to-all-done.3 = f32[1,128,8,4,128]{4,2,3,0,1:T(8,128)} async-done(((f32[1,128,8,4,128]{4,2,3,0,1:T(8,128)}), f32[1,128,8,4,128]{4,2,3,0,1:T(8,128)}, u32[]{:S(2)}, u32[]{:S(2)}) %all-to-all-start.3) | async-done | bytes 2097184 | tf_op jit(solution)/shard_map/all_to_all | solution.py:152
  (568 shorter events, 241.9 us)
Async XLA Ops:
  6.5 1.6 copy-start
  6.5 30.2 %copy-start.15 = (s32[32]{0:T(128)S(1)}, s32[32]{0:T(128)}, u32[]{:S(2)}) copy-start(s32[32]{0:T(128)} %param.19) | copy-start | bytes 388
  6.5 131.3 %all-gather.2.cloned.1.call-start = ((), (), s32[]{:S(2)}) async-start(), calls=%async_computation.6 | async-start | bytes 2228224 | tf_op jit(solution)/shard_map/all_gather | solution.py:110
  38.1 21.3 %copy-start.6 = (bf16[64,2048]{1,0:T(8,128)(2,1)S(1)}, bf16[64,2048]{1,0:T(8,128)(2,1)}, u32[]{:S(2)}) copy-start(bf16[64,2048]{1,0:T(8,128)(2,1)} %param.16) | copy-start | bytes 786436
  140.6 1.6 copy-start.14
  264.1 2.5 copy-start.7
  265.6 1.0 copy-start.3
  272.2 184.6 %all-to-all-start.1 = ((f32[1,128,8,4]{2,3,0,1:T(4,128)}), f32[1,128,8,4]{2,3,0,1:T(4,128)S(1)}, u32[]{:S(2)}, u32[]{:S(2)}) async-start(f32[1,128,8,4]{2,3,0,1:T(4,128)} %bitcast.19), calls=%async_computation.1 | async-start | bytes 524288 | tf_op jit(solution)/shard_map/all_to_all | solution.py:150
  453.5 62.1 %copy-start.4 = (f32[8,8,8,128]{3,1,2,0:T(8,128)S(1)}, f32[8,8,8,128]{3,1,2,0:T(8,128)}, u32[]{:S(2)}) copy-start(f32[8,8,8,128]{3,1,2,0:T(8,128)} %get-tuple-element.312) | copy-start | bytes 786436
  456.8 54.3 %all-to-all-start.2 = ((f32[1,128,8,4]{2,3,0,1:T(4,128)}), f32[1,128,8,4]{2,3,0,1:T(4,128)S(1)}, u32[]{:S(2)}, u32[]{:S(2)}) async-start(f32[1,128,8,4]{2,3,0,1:T(4,128)} %bitcast.22), calls=%async_computation.2 | async-start | bytes 524288 | tf_op jit(solution)/shard_map/all_to_all | solution.py:151
  500.2 30.9 %copy-start.8 = (f32[64,8,8]{0,2,1:T(8,128)S(1)}, f32[64,8,8]{0,2,1:T(8,128)}, u32[]{:S(2)}) copy-start(f32[64,8,8]{0,2,1:T(8,128)} %get-tuple-element.292) | copy-start | bytes 49156
  500.2 30.9 %copy-start.9 = (f32[64,8,8]{0,2,1:T(8,128)S(1)}, f32[64,8,8]{0,2,1:T(8,128)}, u32[]{:S(2)}) copy-start(f32[64,8,8]{0,2,1:T(8,128)} %get-tuple-element.293) | copy-start | bytes 49156
  500.2 30.9 %copy-start.10 = (f32[64,8,8]{0,2,1:T(8,128)S(1)}, f32[64,8,8]{0,2,1:T(8,128)}, u32[]{:S(2)}) copy-start(f32[64,8,8]{0,2,1:T(8,128)} %get-tuple-element.294) | copy-start | bytes 49156
  500.9 14.9 %copy-start.13 = (f32[64,8,8]{0,2,1:T(8,128)S(1)}, f32[64,8,8]{0,2,1:T(8,128)}, u32[]{:S(2)}) copy-start(f32[64,8,8]{0,2,1:T(8,128)} %get-tuple-element.296) | copy-start | bytes 49156
  511.1 15.5 %all-to-all-start.4 = ((f32[1,128,8,4]{2,3,0,1:T(4,128)}), f32[1,128,8,4]{2,3,0,1:T(4,128)S(1)}, u32[]{:S(2)}, u32[]{:S(2)}) async-start(f32[1,128,8,4]{2,3,0,1:T(4,128)} %bitcast.32), calls=%async_computation.4 | async-start | bytes 524288 | tf_op jit(solution)/shard_map/all_to_all | solution.py:150
  526.6 15.5 %all-to-all-start.5 = ((f32[1,128,8,4]{2,3,0,1:T(4,128)}), f32[1,128,8,4]{2,3,0,1:T(4,128)S(1)}, u32[]{:S(2)}, u32[]{:S(2)}) async-start(f32[1,128,8,4]{2,3,0,1:T(4,128)} %bitcast.168), calls=%async_computation.5 | async-start | bytes 524288 | tf_op jit(solution)/shard_map/all_to_all | solution.py:151
  542.0 5.8 copy-start.5
  542.0 6.5 %copy-start.12 = (f32[64,8,8]{0,2,1:T(8,128)S(1)}, f32[64,8,8]{0,2,1:T(8,128)}, u32[]{:S(2)}) copy-start(f32[64,8,8]{0,2,1:T(8,128)} %get-tuple-element.297) | copy-start | bytes 49156
  542.0 6.7 %copy-start.11 = (f32[64,8,8]{0,2,1:T(8,128)S(1)}, f32[64,8,8]{0,2,1:T(8,128)}, u32[]{:S(2)}) copy-start(f32[64,8,8]{0,2,1:T(8,128)} %get-tuple-element.298) | copy-start | bytes 49156
  542.0 7.5 %copy-start.2 = (f32[64,8,8,128]{3,0,2,1:T(8,128)S(1)}, f32[64,8,8,128]{3,0,2,1:T(8,128)}, u32[]{:S(2)}) copy-start(f32[64,8,8,128]{3,0,2,1:T(8,128)} %get-tuple-element.120) | copy-start | bytes 6291460
  542.0 35.2 %all-to-all-start = ((f32[1,128,8,4,128]{4,2,3,0,1:T(8,128)}), f32[1,128,8,4,128]{4,2,3,0,1:T(8,128)}, u32[]{:S(2)}, u32[]{:S(2)}) async-start(f32[1,128,8,4,128]{4,2,3,0,1:T(8,128)} %bitcast.162), calls=%async_computation | async-start | bytes 4194304 | tf_op jit(solution)/shard_map/all_to_all | solution.py:152
  577.2 35.1 %all-to-all-start.3 = ((f32[1,128,8,4,128]{4,2,3,0,1:T(8,128)}), f32[1,128,8,4,128]{4,2,3,0,1:T(8,128)}, u32[]{:S(2)}, u32[]{:S(2)}) async-start(f32[1,128,8,4,128]{4,2,3,0,1:T(8,128)} %bitcast.29), calls=%async_computation.3 | async-start | bytes 4194304 | tf_op jit(solution)/shard_map/all_to_all | solution.py:152
  583.5 31.4 %copy-start.1 = (bf16[2,64,8192]{2,1,0:T(8,128)(2,1)S(1)}, bf16[2,64,8192]{2,1,0:T(8,128)(2,1)}, u32[]{:S(2)}) copy-start(bf16[2,64,8192]{2,1,0:T(8,128)(2,1)} %param.14) | copy-start | bytes 6291460
Sparse Core Ops, SparseCore 0:
  36.8 51.4 all-gather.1
where the time goes:
time: 626 us; the launch traced here: 622 us
  matrix products  144 us (23%)
  local copies, waits for them, and re-layouts  143 us (23%)
  blocking collectives  103 us (16%)
  starting transfers between devices  96.9 us (15%)
  waiting for transfers between devices  72.9 us (12%)
  other arithmetic  44.8 us (7%)
  between operations  14.5 us (2%)
    dot_general x26, matrix products, page_partial(): jnp.einsum('pr,pkgd->rkgd', owned_float, per_page, precision=lax.Precisio...  92.9 us
    psum x1, blocking collectives, per_device(): fresh = lax.psum(fresh_part, ('group', 'lend')).astype(jnp.bfloat16)  75.7 us
    all_to_all x2, starting transfers between devices, per_device(): lax.all_to_all(totals, ('group', 'lend'), split_axis=1, concat_axis=0, ti...  48 us
    gather x26, local copies, waits for them, and re-layouts, page_partial(): chosen = jnp.take(queries, owners, axis=0)  46.4 us
    all_to_all x2, waiting for transfers between devices, per_device(): lax.all_to_all(weighted, ('group', 'lend'), split_axis=1, concat_axis=0,...  46.3 us
    all_to_all x2, starting transfers between devices, per_device(): lax.all_to_all(maxima, ('group', 'lend'), split_axis=1, concat_axis=0, ti...  37.5 us
    slice x26, local copies, waits for them, and re-layouts, page_partial(): page_rows[:, 1].reshape(count, PAGE, KVH, HD).astype(jnp.float32)  33.3 us
    psum x1, blocking collectives, per_device(): query_sum = lax.psum(query_part, 'group').astype(jnp.bfloat16)  27 us
  transfers between devices with their start and end apart: 7, of which 5 were waited for; matrix products, arithmetic and copies ran while one was open for 31% of the time, Pallas kernels for 0%

commit v1 on v0

v1 whole, which is shorter than its diff:
```python
import functools

import jax
import jax.numpy as jnp
from jax import lax
from jax.experimental import pallas as pl
from jax.experimental.pallas import tpu as pltpu
from jax.sharding import PartitionSpec as P

HD = 128
CORES = 2
NEG = -1e30
LOG2E = 1.4426950408889634
MESH = pl.DeviceIdType.MESH
F32 = jnp.float32
BF16 = jnp.bfloat16
UNROLL = 8

(S_KVW, S_OWN, S_RS, S_FRS, S_KEY, S_VAL, S_G1, S_G2, S_H1, S_H2, S_SIB,
 S_E, S_EL, S_F, S_FL) = range(15)
L_TOK, L_WQ, L_KV, L_PAGES = range(4)


def kernel(ng, nl, tok, wq, kvw, pages, own_s, len_s, out,
           tok_v, wq_v, wkv_v, pages_v, qpart, rs, fpart, frs, kvown, kv_r, q_all,
           own_b, eo, slot_o, res, res_l, er, el, ff, fb, fl, fr, frl, qf,
           send, recv, local):
    g = lax.axis_index("group")
    l = lax.axis_index("lend")
    y, c = g // CORES, g % CORES
    ny = ng // CORES
    h_own, par = l // 2, l % 2
    kvh = nl // 2
    nch = 2 * ng
    slots = pages.shape[0]
    page = pages.shape[2]
    steps, req, rows = tok_v.shape
    kvrows = kvw.shape[0]

    def copy(src, dst, which, gg, ll):
        return pltpu.make_async_remote_copy(
            src_ref=src, dst_ref=dst, send_sem=send.at[which], recv_sem=recv.at[which],
            device_id=(gg, ll), device_id_type=MESH)

    def wait_all(ref, sem):
        pltpu.make_async_copy(ref, ref, sem).wait()

    def each(n, body):
        def step(k, carry):
            body(k)
            return carry
        lax.fori_loop(1, n, step, 0)

    c_tok = pltpu.make_async_copy(tok.at[:, :, pl.ds(pl.multiple_of(g * rows, 128), rows)], tok_v, local.at[L_TOK])
    c_tok.start()
    c_wq = pltpu.make_async_copy(wq, wq_v, local.at[L_WQ])
    c_wq.start()
    c_kv = pltpu.make_async_copy(
        kvw.at[:, pl.ds(pl.multiple_of(l * HD, HD), HD)],
        wkv_v.at[pl.ds(pl.multiple_of(l * kvrows, kvrows), kvrows)], local.at[L_KV])
    c_kv.start()

    barrier = pltpu.get_barrier_semaphore()

    def greet(gg, ll):
        pl.semaphore_signal(barrier, inc=1, device_id=(gg, ll), device_id_type=MESH)

    each(nl, lambda k: greet(g, lax.rem(l + k, nl)))

    def greet_group(k):
        gg = lax.rem(g + k, ng)
        greet(gg, l)
        greet(gg, h_own * 2 + (1 - par))
    each(ng, greet_group)

    def start_pages(k, carry):
        pltpu.make_async_copy(pages.at[pl.ds(k * 2, 2)], pages_v.at[pl.ds(k * 2, 2)], local.at[L_PAGES]).start()
        return carry
    lax.fori_loop(0, slots // 2, start_pages, 0)

    lane = lax.broadcasted_iota(jnp.int32, (8, 128), 1)
    quarter = (l % 4) * slots
    owners = jnp.full((8, 128), -1, jnp.int32)
    for p in range(slots):
        owners = jnp.where(lane == quarter + p, own_s[p], owners)
    own_b[...] = owners
    eo[l] = owners

    pl.semaphore_wait(barrier, (nl - 1) + 2 * (ng - 1))

    def send_kv(k):
        ll = lax.rem(l + k, nl)
        copy(kvw.at[:, pl.ds(pl.multiple_of(ll * HD, HD), HD)],
             wkv_v.at[pl.ds(pl.multiple_of(l * kvrows, kvrows), kvrows)], S_KVW, g, ll).start()
        copy(own_b, eo.at[l], S_OWN, g, ll).start()
    each(nl, send_kv)

    c_tok.wait()
    tokens = tok_v[...].reshape(steps * req, rows)
    to = lax.broadcasted_iota(jnp.int32, (steps * req, steps * req), 0)
    fro = lax.broadcasted_iota(jnp.int32, (steps * req, steps * req), 1)
    source = ((to // 4) % 2) * req + (to // 8) * 4 + to % 4
    order = jnp.where(fro == source, 1.0, 0.0).astype(BF16)
    ordered = jnp.dot(order, tokens, preferred_element_type=F32).astype(BF16)
    c_wq.wait()
    part = jnp.dot(ordered, wq_v[...], preferred_element_type=F32)
    qpart[...] = part.reshape(nch, 8, 4 * HD)
    mine = g * 2 + par
    rs[mine] = qpart[mine]

    def send_rs(k):
        idx = lax.rem(mine + k, nch)
        copy(qpart.at[idx], rs.at[mine], S_RS, idx // 2, h_own * 2 + idx % 2).start()
    each(nch, send_rs)

    c_kv.wait()
    wait_all(wkv_v.at[pl.ds(0, (nl - 1) * kvrows)], recv.at[S_KVW])
    fpart[...] = jnp.dot(tokens, wkv_v[...], preferred_element_type=F32).reshape(steps, req, HD)
    frs[g] = fpart[:, pl.ds(pl.multiple_of(g * 8, 8), 8), :]

    def send_frs(k):
        gg = lax.rem(g + k, ng)
        copy(fpart.at[:, pl.ds(pl.multiple_of(gg * 8, 8), 8), :], frs.at[g], S_FRS, gg, l).start()
    each(ng, send_frs)

    wait_all(rs.at[pl.ds(0, nch - 1)], recv.at[S_RS])
    blocks = []
    for half in range(2):
        total = rs[half]
        for gg in range(1, ng):
            total = total + rs[2 * gg + half]
        for j in range(4):
            blocks.append(total[:, j * HD:(j + 1) * HD])
    stacked = jnp.concatenate(blocks, axis=0).astype(BF16)
    to = lax.broadcasted_iota(jnp.int32, (64, 64), 0)
    fro = lax.broadcasted_iota(jnp.int32, (64, 64), 1)
    source = ((to // 8) % 2) * 32 + (to % 4) * 8 + ((to // 4) % 2) * 4 + to // 16
    order = jnp.where(fro == source, 1.0, 0.0).astype(BF16)
    chunk = jnp.dot(order, stacked, preferred_element_type=F32).astype(BF16)
    first = 8 * c + 4 * par
    q_all[h_own, y, pl.ds(first, 4)] = chunk.reshape(4, 16, HD)

    piece1 = q_all.at[h_own, y, pl.ds(first, 2)]
    piece2 = q_all.at[h_own, y, pl.ds(first + 2, 2)]

    def send_g2(k):
        copy(piece2, piece2, S_G2, lax.rem(y + k, ny) * CORES + c, l).start()
    each(ny, send_g2)

    def send_g1(k):
        copy(piece1, piece1, S_G1, g, lax.rem(l + k, nl)).start()
    each(nl, send_g1)

    wait_all(q_all.at[pl.ds(0, 2), 0, pl.ds(0, ny - 1)], recv.at[S_G2])

    def send_h2(k):
        block = q_all.at[h_own, :, pl.ds(first + 2, 2)]
        copy(block, block, S_H2, g, lax.rem(l + k, nl)).start()
    each(nl, send_h2)

    wait_all(q_all.at[pl.ds(0, 2), 0, pl.ds(0, nl - 1)], recv.at[S_G1])

    def send_h1(k):
        gg = lax.rem(y + k, ny) * CORES + c
        for pp in range(2):
            block = q_all.at[:, y, pl.ds(8 * c + 4 * pp, 2)]
            copy(block, block, S_H1, gg, l).start()
    each(ny, send_h1)

    wait_all(frs.at[pl.ds(0, ng - 1)], recv.at[S_FRS])
    total = frs[0]
    for gg in range(1, ng):
        total = total + frs[gg]
    kvown[...] = total.reshape(steps * 8, HD).astype(BF16)
    which = l // kvh
    for pp in range(2):
        ll = (l % kvh) * 2 + pp

        @pl.when(ll == l)
        def _():
            kv_r[which] = kvown[...]

        for kind in range(2):
            @pl.when((ll != l) & (which == kind))
            def _():
                copy(kvown, kv_r.at[kind], S_KEY + kind, g, ll).start()

    wait_all(q_all.at[:, pl.ds(0, ny - 1), pl.ds(0, 4)], recv.at[S_H1])
    for pp in range(2):
        block = q_all.at[:, :, pl.ds(8 * c + 4 * pp, 2)]
        copy(block, block, S_SIB, y * CORES + (1 - c), l).start()
    wait_all(q_all.at[:, 0, pl.ds(0, (nl - 1) * ny * 2 // kvh)], recv.at[S_H2])
    for pp in range(2):
        block = q_all.at[:, :, pl.ds(8 * c + 4 * pp + 2, 2)]
        copy(block, block, S_SIB, y * CORES + (1 - c), l).start()
    wait_all(q_all.at[:, :, pl.ds(0, 8)], recv.at[S_SIB])
    wait_all(pages_v, local.at[L_PAGES])

    scale = LOG2E / (HD ** 0.5)
    lane16 = lax.broadcasted_iota(jnp.int32, (16, 128), 1)

    def head(i, carry):
        h = lax.rem(h_own + 1 + i, kvh)
        columns = pl.ds(pl.multiple_of(h * HD, HD), HD)

        def visit(b, state):
            maxima, sums = state
            for u in range(UNROLL):
                p = b * UNROLL + u
                r = own_s[p]
                query = q_all[h, r // 16, r % 16]
                keys = pages_v[p, 0, :, columns]
                values = pages_v[p, 1, :, columns]
                s = lax.dot_general(query, keys, (((1,), (1,)), ((), ())), preferred_element_type=F32) * scale
                ok = lane16 < len_s[p]
                s = jnp.where(ok, s, NEG)
                m = jnp.max(s, axis=1, keepdims=True)
                w = jnp.where(ok, jnp.exp2(s - m), 0.0)
                t = jnp.sum(w, axis=1, keepdims=True)
                o = jnp.dot(w.astype(BF16), values, preferred_element_type=F32)
                o = o / jnp.maximum(t, 1e-30)
                slot_o[pl.ds(p, 16, stride=slots), :] = o
                here = lane16 == quarter + p
                maxima = jnp.where(here, m, maxima)
                sums = jnp.where(here, t, sums)
            return maxima, sums

        maxima, sums = lax.fori_loop(
            0, slots // UNROLL, visit,
            (jnp.full((16, 128), NEG, F32), jnp.zeros((16, 128), F32)))
        lse = jnp.where(sums > 0.0, maxima + jnp.log(jnp.maximum(sums, 1e-30)) * LOG2E, NEG)
        for half in range(2):
            ll = 2 * h + half
            res[ll] = slot_o[pl.ds(half * 8 * slots, 8 * slots), :].astype(BF16)
            res_l[ll] = lse[half * 8:(half + 1) * 8]

            @pl.when(ll != l)
            def _():
                copy(res.at[ll], er.at[l], S_E, g, ll).start()
                copy(res_l.at[ll], el.at[l], S_EL, g, ll).start()

            @pl.when(ll == l)
            def _():
                er[l] = res[ll]
                el[l] = res_l[ll]
        return carry

    lax.fori_loop(0, kvh, head, 0)

    qf[...] = q_all[h_own, y, pl.ds(8 * c, 8)].reshape(128, HD).astype(F32)

    @pl.when(l != h_own)
    def _():
        wait_all(kv_r.at[0], recv.at[S_KEY])

    @pl.when(l != kvh + h_own)
    def _():
        wait_all(kv_r.at[1], recv.at[S_VAL])

    fresh_k = kv_r[0].astype(F32)
    fresh_v = kv_r[1].astype(F32)
    fresh_scores = []
    for i in range(8):
        q_i = qf[pl.ds(par * 8 + i, 8, stride=16), :]
        fresh_scores.append([
            jnp.sum(q_i * fresh_k[t * 8:(t + 1) * 8], axis=1, keepdims=True) * scale
            for t in range(i // 4 + 1)])

    wait_all(eo.at[pl.ds(0, nl - 1)], recv.at[S_OWN])
    wait_all(el.at[pl.ds(0, nl - 1)], recv.at[S_EL])
    wait_all(er.at[pl.ds(0, nl - 1)], recv.at[S_E])
    request = lax.broadcasted_iota(jnp.int32, (req, 128), 0)
    owned, logs = [], []
    for k in range(nl // 4):
        o, s = eo[4 * k], el[4 * k]
        for x in range(1, 4):
            o = jnp.maximum(o, eo[4 * k + x])
            s = jnp.maximum(s, el[4 * k + x])
        owned.append(o[0:1] == request)
        logs.append(s)
    laneq = lax.broadcasted_iota(jnp.int32, (req, 128), 1)
    lse_out = jnp.full((req, 128), NEG, F32)
    for i in range(8):
        masked = [jnp.where(owned[k], logs[k][i:i + 1], NEG) for k in range(nl // 4)]
        m = masked[0]
        for k in range(1, nl // 4):
            m = jnp.maximum(m, masked[k])
        m = jnp.max(m, axis=1, keepdims=True)
        weights = [jnp.where(x > 0.5 * NEG, jnp.exp2(x - m), 0.0) for x in masked]
        t = weights[0]
        for k in range(1, nl // 4):
            t = t + weights[k]
        t = jnp.sum(t, axis=1, keepdims=True)
        weights = jnp.concatenate(weights, axis=1).astype(BF16)
        data = er[:, i * slots:(i + 1) * slots, :].reshape(nl * slots, HD)
        o = jnp.dot(weights, data, preferred_element_type=F32) / jnp.maximum(t, 1e-30)
        ff[:, i * 8:(i + 1) * 8, :] = o.reshape(ng, 8, HD)
        lse = jnp.where(t > 0.0, m + jnp.log(jnp.maximum(t, 1e-30)) * LOG2E, NEG)
        lse_out = jnp.where(laneq == i, lse, lse_out)
    fb[...] = ff[...].astype(BF16)
    fl[...] = lse_out.reshape(ng, 8, 128)
    fr[g] = fb[g]
    frl[g] = fl[g]

    def send_f(k):
        gg = lax.rem(g + k, ng)
        copy(fb.at[gg], fr.at[g], S_F, gg, l).start()
        copy(fl.at[gg], frl.at[g], S_FL, gg, l).start()
    each(ng, send_f)

    wait_all(frl.at[pl.ds(0, ng - 1)], recv.at[S_FL])
    wait_all(fr.at[pl.ds(0, ng - 1)], recv.at[S_F])
    data = [fr[gg].astype(F32) for gg in range(ng)]
    logs = [frl[gg] for gg in range(ng)]
    for s in range(steps):
        pieces = []
        for j in range(4):
            i = s * 4 + j
            parts = [(logs[gg][:, i:i + 1], data[gg][i * 8:(i + 1) * 8]) for gg in range(ng)]
            parts += [(fresh_scores[i][t], fresh_v[t * 8:(t + 1) * 8]) for t in range(s + 1)]
            m = parts[0][0]
            for score, unused in parts[1:]:
                m = jnp.maximum(m, score)
            total = jnp.zeros((8, 1), F32)
            o = jnp.zeros((8, HD), F32)
            for score, value in parts:
                w = jnp.exp2(score - m)
                total = total + w
                o = o + w * value
            pieces.append(o / total)
        out[s] = jnp.concatenate(pieces, axis=1).astype(BF16)

    wait_all(wkv_v.at[pl.ds(0, (nl - 1) * kvrows)], send.at[S_KVW])
    wait_all(eo.at[pl.ds(0, nl - 1)], send.at[S_OWN])
    wait_all(rs.at[pl.ds(0, nch - 1)], send.at[S_RS])
    wait_all(frs.at[pl.ds(0, ng - 1)], send.at[S_FRS])
    wait_all(q_all.at[pl.ds(0, 2), 0, pl.ds(0, nl - 1)], send.at[S_G1])
    wait_all(q_all.at[pl.ds(0, 2), 0, pl.ds(0, ny - 1)], send.at[S_G2])
    wait_all(q_all.at[:, pl.ds(0, ny - 1), pl.ds(0, 4)], send.at[S_H1])
    wait_all(q_all.at[:, 0, pl.ds(0, (nl - 1) * ny * 2 // kvh)], send.at[S_H2])
    wait_all(q_all.at[:, :, pl.ds(0, 8)], send.at[S_SIB])
    for kind in range(2):
        for pp in range(2):
            @pl.when((which == kind) & ((l % kvh) * 2 + pp != l))
            def _():
                wait_all(kvown, send.at[S_KEY + kind])
    wait_all(er.at[pl.ds(0, nl - 1)], send.at[S_E])
    wait_all(el.at[pl.ds(0, nl - 1)], send.at[S_EL])
    wait_all(fr.at[pl.ds(0, ng - 1)], send.at[S_F])
    wait_all(frl.at[pl.ds(0, ng - 1)], send.at[S_FL])


def per_device(ng, nl, tokens, query_weight, kv_weight, pages, slot_request, slot_len):
    steps, req, width = tokens.shape
    rows = query_weight.shape[0]
    slots, unused, page, kvwidth = pages.shape
    kvh = kvwidth // HD
    ny = ng // CORES
    hbm = pl.BlockSpec(memory_space=pl.ANY)
    smem = pl.BlockSpec(memory_space=pltpu.SMEM)
    scratch = [
        pltpu.VMEM((steps, req, rows), BF16),
        pltpu.VMEM((rows, 4 * HD), BF16),
        pltpu.VMEM((rows, HD), BF16),
        pltpu.VMEM(pages.shape, BF16),
        pltpu.VMEM((2 * ng, 8, 4 * HD), F32),
        pltpu.VMEM((2 * ng, 8, 4 * HD), F32),
        pltpu.VMEM((steps, req, HD), F32),
        pltpu.VMEM((ng, steps, 8, HD), F32),
        pltpu.VMEM((steps * 8, HD), BF16),
        pltpu.VMEM((2, steps * 8, HD), BF16),
        pltpu.VMEM((kvh, ny, 16, 16, HD), BF16),
        pltpu.VMEM((8, 128), jnp.int32),
        pltpu.VMEM((nl, 8, 128), jnp.int32),
        pltpu.VMEM((16 * slots, HD), F32),
        pltpu.VMEM((nl, 8 * slots, HD), BF16),
        pltpu.VMEM((nl, 8, 128), F32),
        pltpu.VMEM((nl, 8 * slots, HD), BF16),
        pltpu.VMEM((nl, 8, 128), F32),
        pltpu.VMEM((ng, 64, HD), F32),
        pltpu.VMEM((ng, 64, HD), BF16),
        pltpu.VMEM((ng, 8, 128), F32),
        pltpu.VMEM((ng, 64, HD), BF16),
        pltpu.VMEM((ng, 8, 128), F32),
        pltpu.VMEM((128, HD), F32),
        pltpu.SemaphoreType.DMA((15,)),
        pltpu.SemaphoreType.DMA((15,)),
        pltpu.SemaphoreType.DMA((4,)),
    ]
    return pl.pallas_call(
        functools.partial(kernel, ng, nl),
        out_shape=jax.ShapeDtypeStruct((steps, req // ng, 4 * HD), BF16),
        in_specs=[hbm, hbm, hbm, hbm, smem, smem],
        out_specs=pl.BlockSpec(memory_space=pltpu.VMEM),
        scratch_shapes=scratch,
        compiler_params=pltpu.CompilerParams(
            collective_id=0, has_side_effects=True, vmem_limit_bytes=48 * 1024 * 1024),
    )(tokens, query_weight, kv_weight, pages, slot_request, slot_len)


def solution(mesh):
    ng, nl = mesh.shape["group"], mesh.shape["lend"]
    return jax.shard_map(
        functools.partial(per_device, ng, nl),
        mesh=mesh,
        in_specs=(
            P(),
            P("group", "lend"),
            P(("group", "lend"), None),
            P(("group", "lend"), None, None, None),
            P(("group", "lend")),
            P(("group", "lend")),
        ),
        out_specs=P(None, "group", "lend"),
        check_vma=False,
    )
```

time: 626 us -> 110 us (0.18)
  matrix products: 144 us -> 0 us
  local copies, waits for them, and re-layouts: 143 us -> 5.68 us
  Pallas kernels: 0 us -> 104 us
  blocking collectives: 103 us -> 0 us
  starting transfers between devices: 96.9 us -> 0 us
  waiting for transfers between devices: 72.9 us -> 0 us
  other arithmetic: 44.8 us -> 0 us
  between operations: 14.5 us -> 0.01 us
    dot_general x109 -> x0, matrix products: 144 us -> none  [the longest x26 92.9 us: page_partial(): jnp.einsum('pr,pkgd->rkgd', owned_float, per_page, precision=lax.Precisio...]
    pallas_call x0 -> x1, Pallas kernels: none -> 104 us  [per_device(): pl.pallas_call(functools.partial(kernel, ng, nl), out_shape=jax.ShapeDtyp...]
    psum x2 -> x0, blocking collectives: 103 us -> none  [the longest x1 75.7 us: per_device(): fresh = lax.psum(fresh_part, ('group', 'lend')).astype(jnp.bfloat16)]
    all_to_all x6 -> x0, starting transfers between devices: 96.9 us -> none  [the longest x2 48 us: per_device(): lax.all_to_all(totals, ('group', 'lend'), split_axis=1, concat_axis=0, ti...]
    all_to_all x6 -> x0, waiting for transfers between devices: 72.8 us -> none  [the longest x2 46.3 us: per_device(): lax.all_to_all(weighted, ('group', 'lend'), split_axis=1, concat_axis=0,...]
    gather x52 -> x0, local copies, waits for them, and re-layouts: 60.6 us -> none  [the longest x26 46.4 us: page_partial(): chosen = jnp.take(queries, owners, axis=0)]
    slice x27 -> x0, local copies, waits for them, and re-layouts: 34 us -> none  [the longest x26 33.3 us: page_partial(): page_rows[:, 1].reshape(count, PAGE, KVH, HD).astype(jnp.float32)]
    and x78 -> x0, other arithmetic: 22.2 us -> none  [the longest x26 18.3 us: page_partial(): chosen = jnp.take(queries, owners, axis=0)]
  transfers between devices with their start and end apart: 7 -> 0, of which waited for: 5 -> 0; matrix products, arithmetic and copies ran while one was open for 31% -> 0% of each run, Pallas kernels for 0% -> 0%
where the time goes in v1:
time: 110 us; the launch traced here: 109 us
  Pallas kernels  104 us (95%)
  local copies, waits for them, and re-layouts  5.68 us (5%)
    pallas_call x1, Pallas kernels, per_device(): pl.pallas_call(functools.partial(kernel, ng, nl), out_shape=jax.ShapeDtyp...  104 us
    unnamed x11, local copies, waits for them, and re-layouts  5.68 us

profile of v1, /device:TPU:1, one launch (start us, length us, event | category | flops | bytes accessed | tf_op | source)
XLA Modules:
  0.0 109.4 jit_solution(667527905742018461)
XLA Ops:
  0.0 0.0 copy-start
  0.0 1.6 %copy-done = bf16[2,64,8192]{2,1,0:T(8,128)(2,1)S(1)} copy-done((bf16[2,64,8192]{2,1,0:T(8,128)(2,1)S(1)}, bf16[2,64,8192]{2,1,0:T(8,128)(2,1)}, u32[]{:S(2)}) %copy-start) | copy-done | bytes 2097176
  1.6 0.0 copy-start.1
  1.6 1.2 %copy-done.1 = bf16[1024,512]{1,0:T(8,128)(2,1)S(1)} copy-done((bf16[1024,512]{1,0:T(8,128)(2,1)S(1)}, bf16[1024,512]{1,0:T(8,128)(2,1)}, u32[]{:S(2)}) %copy-start.1) | copy-done | bytes 1048600
  2.8 0.0 copy-start.2
  2.8 0.9 copy-done.2
  3.8 0.0 copy-start.3
  3.8 0.7 copy-done.3
  4.4 0.0 copy-start.4
  4.4 0.7 copy-done.4
  5.1 103.7 %shard_map.64 = bf16[2,8,512]{2,1,0:T(8,128)(2,1)S(1)} custom-call(bf16[2,64,8192]{2,1,0:T(8,128)(2,1)S(1)} %copy-done, bf16[1024,512]{1,0:T(8,128)(2,1)S(1)} %copy-done.1, bf16[64,2048]{1,0:T(8,128)(2,1)S(1)} %copy-done.2, bf16[32,2,128,1024]{3,2,1,0:T(8,128)(2,1)} %pages.1, s32[32]{0:T(128)S(1)} %copy-done.3, s32[32]{0:T(128)S(1)} %copy-done.4), custom_call_target="tpu_custom_call" | custom-call | tf_op jit(solution)/shard_map/pallas_call | solution.py:390
  108.7 0.6 copy.8
Async XLA Ops:
  0.0 1.6 %copy-start = (bf16[2,64,8192]{2,1,0:T(8,128)(2,1)S(1)}, bf16[2,64,8192]{2,1,0:T(8,128)(2,1)}, u32[]{:S(2)}) copy-start(bf16[2,64,8192]{2,1,0:T(8,128)(2,1)} %tok.1) | copy-start | bytes 6291460
  1.6 1.2 %copy-start.1 = (bf16[1024,512]{1,0:T(8,128)(2,1)S(1)}, bf16[1024,512]{1,0:T(8,128)(2,1)}, u32[]{:S(2)}) copy-start(bf16[1024,512]{1,0:T(8,128)(2,1)} %wq.1) | copy-start | bytes 3145732
  2.8 0.9 copy-start.2
  3.8 0.7 copy-start.3
  4.4 0.7 copy-start.4

commit v2 on v1

--- a/solution.py
+++ b/solution.py
@@ -14,7 +14,7 @@
 MESH = pl.DeviceIdType.MESH
 F32 = jnp.float32
 BF16 = jnp.bfloat16
-UNROLL = 8
+UNROLL = 16
 
 (S_KVW, S_OWN, S_RS, S_FRS, S_KEY, S_VAL, S_G1, S_G2, S_H1, S_H2, S_SIB,
  S_E, S_EL, S_F, S_FL) = range(15)
@@ -78,23 +78,6 @@
         return carry
     lax.fori_loop(0, slots // 2, start_pages, 0)
 
-    lane = lax.broadcasted_iota(jnp.int32, (8, 128), 1)
-    quarter = (l % 4) * slots
-    owners = jnp.full((8, 128), -1, jnp.int32)
-    for p in range(slots):
-        owners = jnp.where(lane == quarter + p, own_s[p], owners)
-    own_b[...] = owners
-    eo[l] = owners
-
-    pl.semaphore_wait(barrier, (nl - 1) + 2 * (ng - 1))
-
-    def send_kv(k):
-        ll = lax.rem(l + k, nl)
-        copy(kvw.at[:, pl.ds(pl.multiple_of(ll * HD, HD), HD)],
-             wkv_v.at[pl.ds(pl.multiple_of(l * kvrows, kvrows), kvrows)], S_KVW, g, ll).start()
-        copy(own_b, eo.at[l], S_OWN, g, ll).start()
-    each(nl, send_kv)
-
     c_tok.wait()
     tokens = tok_v[...].reshape(steps * req, rows)
     to = lax.broadcasted_iota(jnp.int32, (steps * req, steps * req), 0)
@@ -108,20 +91,18 @@
     mine = g * 2 + par
     rs[mine] = qpart[mine]
 
+    pl.semaphore_wait(barrier, (nl - 1) + 2 * (ng - 1))
+
     def send_rs(k):
         idx = lax.rem(mine + k, nch)
         copy(qpart.at[idx], rs.at[mine], S_RS, idx // 2, h_own * 2 + idx % 2).start()
     each(nch, send_rs)
 
-    c_kv.wait()
-    wait_all(wkv_v.at[pl.ds(0, (nl - 1) * kvrows)], recv.at[S_KVW])
-    fpart[...] = jnp.dot(tokens, wkv_v[...], preferred_element_type=F32).reshape(steps, req, HD)
-    frs[g] = fpart[:, pl.ds(pl.multiple_of(g * 8, 8), 8), :]
-
-    def send_frs(k):
-        gg = lax.rem(g + k, ng)
-        copy(fpart.at[:, pl.ds(pl.multiple_of(gg * 8, 8), 8), :], frs.at[g], S_FRS, gg, l).start()
-    each(ng, send_frs)
+    def send_kv(k):
+        ll = lax.rem(l + k, nl)
+        copy(kvw.at[:, pl.ds(pl.multiple_of(ll * HD, HD), HD)],
+             wkv_v.at[pl.ds(pl.multiple_of(l * kvrows, kvrows), kvrows)], S_KVW, g, ll).start()
+    each(nl, send_kv)
 
     wait_all(rs.at[pl.ds(0, nch - 1)], recv.at[S_RS])
     blocks = []
@@ -151,6 +132,16 @@
         copy(piece1, piece1, S_G1, g, lax.rem(l + k, nl)).start()
     each(nl, send_g1)
 
+    c_kv.wait()
+    wait_all(wkv_v.at[pl.ds(0, (nl - 1) * kvrows)], recv.at[S_KVW])
+    fpart[...] = jnp.dot(tokens, wkv_v[...], preferred_element_type=F32).reshape(steps, req, HD)
+    frs[g] = fpart[:, pl.ds(pl.multiple_of(g * 8, 8), 8), :]
+
+    def send_frs(k):
+        gg = lax.rem(g + k, ng)
+        copy(fpart.at[:, pl.ds(pl.multiple_of(gg * 8, 8), 8), :], frs.at[g], S_FRS, gg, l).start()
+    each(ng, send_frs)
+
     wait_all(q_all.at[pl.ds(0, 2), 0, pl.ds(0, ny - 1)], recv.at[S_G2])
 
     def send_h2(k):
@@ -166,6 +157,25 @@
             block = q_all.at[:, y, pl.ds(8 * c + 4 * pp, 2)]
             copy(block, block, S_H1, gg, l).start()
     each(ny, send_h1)
+
+    lane = lax.broadcasted_iota(jnp.int32, (8, 128), 1)
+    quarter = (l % 4) * slots
+    owners = jnp.full((8, 128), -1, jnp.int32)
+    for p in range(slots):
+        owners = jnp.where(lane == quarter + p, own_s[p], owners)
+    own_b[...] = owners
+    eo[l] = owners
+
+    each(nl, lambda k: copy(own_b, eo.at[l], S_OWN, g, lax.rem(l + k, nl)).start())
+
+    wait_all(q_all.at[:, pl.ds(0, ny - 1), pl.ds(0, 4)], recv.at[S_H1])
+    for pp in range(2):
+        block = q_all.at[:, :, pl.ds(8 * c + 4 * pp, 2)]
+        copy(block, block, S_SIB, y * CORES + (1 - c), l).start()
+    wait_all(q_all.at[:, 0, pl.ds(0, (nl - 1) * ny * 2 // kvh)], recv.at[S_H2])
+    for pp in range(2):
+        block = q_all.at[:, :, pl.ds(8 * c + 4 * pp + 2, 2)]
+        copy(block, block, S_SIB, y * CORES + (1 - c), l).start()
 
     wait_all(frs.at[pl.ds(0, ng - 1)], recv.at[S_FRS])
     total = frs[0]
@@ -185,14 +195,6 @@
             def _():
                 copy(kvown, kv_r.at[kind], S_KEY + kind, g, ll).start()
 
-    wait_all(q_all.at[:, pl.ds(0, ny - 1), pl.ds(0, 4)], recv.at[S_H1])
-    for pp in range(2):
-        block = q_all.at[:, :, pl.ds(8 * c + 4 * pp, 2)]
-        copy(block, block, S_SIB, y * CORES + (1 - c), l).start()
-    wait_all(q_all.at[:, 0, pl.ds(0, (nl - 1) * ny * 2 // kvh)], recv.at[S_H2])
-    for pp in range(2):
-        block = q_all.at[:, :, pl.ds(8 * c + 4 * pp + 2, 2)]
-        copy(block, block, S_SIB, y * CORES + (1 - c), l).start()
     wait_all(q_all.at[:, :, pl.ds(0, 8)], recv.at[S_SIB])
     wait_all(pages_v, local.at[L_PAGES])
 
@@ -205,21 +207,23 @@
 
         def visit(b, state):
             maxima, sums = state
-            for u in range(UNROLL):
-                p = b * UNROLL + u
+            block = [b * UNROLL + u for u in range(UNROLL)]
+            scores = []
+            for p in block:
                 r = own_s[p]
-                query = q_all[h, r // 16, r % 16]
-                keys = pages_v[p, 0, :, columns]
-                values = pages_v[p, 1, :, columns]
-                s = lax.dot_general(query, keys, (((1,), (1,)), ((), ())), preferred_element_type=F32) * scale
-                ok = lane16 < len_s[p]
-                s = jnp.where(ok, s, NEG)
-                m = jnp.max(s, axis=1, keepdims=True)
-                w = jnp.where(ok, jnp.exp2(s - m), 0.0)
-                t = jnp.sum(w, axis=1, keepdims=True)
-                o = jnp.dot(w.astype(BF16), values, preferred_element_type=F32)
-                o = o / jnp.maximum(t, 1e-30)
-                slot_o[pl.ds(p, 16, stride=slots), :] = o
+                scores.append(lax.dot_general(
+                    q_all[h, r // 16, r % 16], pages_v[p, 0, :, columns],
+                    (((1,), (1,)), ((), ())), preferred_element_type=F32) * scale)
+            valid = [lane16 < len_s[p] for p in block]
+            scores = [jnp.where(ok, x, NEG) for ok, x in zip(valid, scores)]
+            tops = [jnp.max(x, axis=1, keepdims=True) for x in scores]
+            weights = [jnp.where(ok, jnp.exp2(x - m), 0.0) for ok, x, m in zip(valid, scores, tops)]
+            totals = [jnp.sum(w, axis=1, keepdims=True) for w in weights]
+            outs = [
+                jnp.dot(w.astype(BF16), pages_v[p, 1, :, columns], preferred_element_type=F32)
+                for w, p in zip(weights, block)]
+            for p, o, m, t in zip(block, outs, tops, totals):
+                slot_o[pl.ds(p, 16, stride=slots), :] = o / jnp.maximum(t, 1e-30)
                 here = lane16 == quarter + p
                 maxima = jnp.where(here, m, maxima)
                 sums = jnp.where(here, t, sums)
@@ -394,7 +398,7 @@
         out_specs=pl.BlockSpec(memory_space=pltpu.VMEM),
         scratch_shapes=scratch,
         compiler_params=pltpu.CompilerParams(
-            collective_id=0, has_side_effects=True, vmem_limit_bytes=48 * 1024 * 1024),
+            collective_id=0, has_side_effects=True, vmem_limit_bytes=62 * 1024 * 1024),
     )(tokens, query_weight, kv_weight, pages, slot_request, slot_len)
 
 

time: 110 us -> 57.8 us (0.53)
  Pallas kernels: 104 us -> 56.3 us
  local copies, waits for them, and re-layouts: 5.68 us -> 1.32 us
    pallas_call x1, Pallas kernels: 104 us -> 56.3 us  [per_device(): pl.pallas_call(functools.partial(kernel, ng, nl), out_shape=jax.ShapeDtyp...]
    unnamed x11 -> x1, local copies, waits for them, and re-layouts: 5.68 us -> 1.32 us
where the time goes in v2:
time: 57.8 us; the launch traced here: 57.6 us
  Pallas kernels  56.3 us (97%)
  local copies, waits for them, and re-layouts  1.32 us (2%)
    pallas_call x1, Pallas kernels, per_device(): pl.pallas_call(functools.partial(kernel, ng, nl), out_shape=jax.ShapeDtyp...  56.3 us
    unnamed x1, local copies, waits for them, and re-layouts  1.32 us

profile of v2, /device:TPU:1, one launch (start us, length us, event | category | flops | bytes accessed | tf_op | source)
XLA Modules:
  0.0 57.6 jit_solution(14775089081097698332)
XLA Ops:
  0.0 56.3 %shard_map.64 = bf16[2,8,512]{2,1,0:T(8,128)(2,1)} custom-call(bf16[2,64,8192]{2,1,0:T(8,128)(2,1)} %tok.1, bf16[1024,512]{1,0:T(8,128)(2,1)} %wq.1, bf16[64,2048]{1,0:T(8,128)(2,1)} %kvw.1, bf16[32,2,128,1024]{3,2,1,0:T(8,128)(2,1)} %pages.1, s32[32]{0:T(128)} %own_s.1, s32[32]{0:T(128)} %len_s.1), custom_call_target="tpu_custom_call" | custom-call | tf_op jit(solution)/shard_map/pallas_call | solution.py:394
  56.3 1.3 %copy.8 = bf16[2,8,512]{2,1,0:T(8,128)(2,1)} copy(bf16[2,8,512]{2,1,0:T(8,128)(2,1)} %shard_map.64) | data formatting | bytes 32768

commit v3 on v2

v3 whole, which is shorter than its diff:
```python
import functools

import jax
import jax.numpy as jnp
from jax import lax
from jax.experimental import pallas as pl
from jax.experimental.pallas import tpu as pltpu
from jax.sharding import PartitionSpec as P

HD = 128
CORES = 2
NEG = -1e30
LOG2E = 1.4426950408889634
MESH = pl.DeviceIdType.MESH
F32 = jnp.float32
BF16 = jnp.bfloat16
UNROLL = 16
SPLIT = 3
AHEAD = 8

(S_KVW, S_RS, S_FRS, S_KEY, S_VAL, S_G1, S_G2, S_H1, S_H2, S_SIB,
 S_E, S_F) = range(12)
H_G1, H_H1, H_H2, H_SIB = range(4)
L_TOK, L_WQ, L_KV, L_PAGES = range(4)


def pieces_of(x):
    hi = x.astype(BF16).astype(F32)
    mid = (x - hi).astype(BF16).astype(F32)
    return hi, mid, x - hi - mid


def kernel(ng, nl, tok, wq, kvw, pages, own_s, len_s, out,
           tok_v, wq_v, wkv_v, pages_v, qpart, rs, fpart, frs, kvown, kv_r, q_all,
           slot_o, res, er, ff, fb, fr, qf, q_head,
           send, recv, by_head, local):
    g = lax.axis_index("group")
    l = lax.axis_index("lend")
    y, c = g // CORES, g % CORES
    ny = ng // CORES
    h_own, par = l // 2, l % 2
    kvh = nl // 2
    nch = 2 * ng
    offsets = (2, 7, 1, 4, 3, 6, 5, 0) if kvh == 8 else tuple(range(kvh - 1, -1, -1))
    table = sum(offset * 8 ** i for i, offset in enumerate(offsets))
    turn = 1 - 2 * par

    def head_at(i):
        offset = (table >> (3 * i)) & 7
        nx = nl // 4
        hx = lax.rem(l // 4 + turn * (offset // 2) + nx, nx)
        return hx * 2 + (h_own + offset) % 2

    slots = pages.shape[0]
    page = pages.shape[2]
    steps, req, rows = tok_v.shape
    kvrows = kvw.shape[0]

    def copy(src, dst, which, gg, ll):
        return pltpu.make_async_remote_copy(
            src_ref=src, dst_ref=dst, send_sem=send.at[which], recv_sem=recv.at[which],
            device_id=(gg, ll), device_id_type=MESH)

    def head_copy(block, which, kind, h, gg, ll):
        return pltpu.make_async_remote_copy(
            src_ref=block, dst_ref=block, send_sem=send.at[which], recv_sem=by_head.at[kind, h],
            device_id=(gg, ll), device_id_type=MESH)

    def wait_all(ref, sem):
        pltpu.make_async_copy(ref, ref, sem).wait()

    def each(n, body):
        def step(k, carry):
            body(k)
            return carry
        lax.fori_loop(1, n, step, 0)

    for s in range(steps):
        pltpu.make_async_copy(
            tok.at[s, :, pl.ds(pl.multiple_of(g * rows, 128), rows)], tok_v.at[s], local.at[L_TOK]).start()
    quarter_rows = rows // 4
    for k in range(4):
        part_rows = pl.ds(k * quarter_rows, quarter_rows)
        pltpu.make_async_copy(wq.at[part_rows], wq_v.at[part_rows], local.at[L_WQ]).start()
    c_kv = pltpu.make_async_copy(
        kvw.at[:, pl.ds(pl.multiple_of(l * HD, HD), HD)],
        wkv_v.at[pl.ds(pl.multiple_of(l * kvrows, kvrows), kvrows)], local.at[L_KV])
    c_kv.start()

    barrier = pltpu.get_barrier_semaphore()

    def greet(gg, ll):
        pl.semaphore_signal(barrier, inc=1, device_id=(gg, ll), device_id_type=MESH)

    each(nl, lambda k: greet(g, lax.rem(l + k, nl)))

    def greet_group(k):
        gg = lax.rem(g + k, ng)
        greet(gg, l)
        greet(gg, h_own * 2 + (1 - par))
    each(ng, greet_group)

    def start_pages(k, carry):
        pltpu.make_async_copy(pages.at[pl.ds(k * 2, 2)], pages_v.at[pl.ds(k * 2, 2)], local.at[L_PAGES]).start()
        return carry
    lax.fori_loop(0, slots // 2, start_pages, 0)

    wait_all(tok_v, local.at[L_TOK])
    tokens = tok_v[...].reshape(steps * req, rows)
    wait_all(wq_v, local.at[L_WQ])
    part = jnp.dot(tokens, wq_v[...], preferred_element_type=F32).reshape(steps, ng, 8, 4 * HD)
    upper = lax.broadcasted_iota(jnp.int32, (8, 4 * HD), 0) < 4
    for gg in range(ng):
        first, second = part[0, gg], part[1, gg]
        qpart[2 * gg] = jnp.where(upper, first, pltpu.roll(second, 4, 0))
        qpart[2 * gg + 1] = jnp.where(upper, pltpu.roll(first, 4, 0), second)
    mine = g * 2 + par
    rs[mine] = qpart[mine]

    pl.semaphore_wait(barrier, (nl - 1) + 2 * (ng - 1))

    def send_rs(k):
        idx = lax.rem(mine + k, nch)
        copy(qpart.at[idx], rs.at[mine], S_RS, idx // 2, h_own * 2 + idx % 2).start()
    each(nch, send_rs)

    wait_all(rs.at[pl.ds(0, nch - 1)], recv.at[S_RS])
    blocks = []
    for half in range(2):
        total = rs[half]
        for gg in range(1, ng):
            total = total + rs[2 * gg + half]
        for j in range(4):
            blocks.append(total[:, j * HD:(j + 1) * HD])
    stacked = jnp.concatenate(blocks, axis=0).astype(BF16)
    to = lax.broadcasted_iota(jnp.int32, (64, 64), 0)
    fro = lax.broadcasted_iota(jnp.int32, (64, 64), 1)
    source = ((to // 8) % 2) * 32 + (to % 4) * 8 + ((to // 4) % 2) * 4 + to // 16
    order = jnp.where(fro == source, 1.0, 0.0).astype(BF16)
    chunk = jnp.dot(order, stacked, preferred_element_type=F32).astype(BF16)
    for r4 in range(4):
        q_all[h_own, y, c, r4, par] = chunk[r4 * 16:(r4 + 1) * 16]

    piece1 = q_all.at[h_own, y, c, pl.ds(0, SPLIT), par]
    piece2 = q_all.at[h_own, y, c, pl.ds(SPLIT, 4 - SPLIT), par]

    def send_g2(k):
        copy(piece2, piece2, S_G2, lax.rem(y + k, ny) * CORES + c, l).start()
    each(ny, send_g2)

    def send_g1(k):
        head_copy(piece1, S_G1, H_G1, h_own, g, lax.rem(l + nl - k, nl)).start()
    each(nl, send_g1)

    def send_kv(k):
        ll = lax.rem(l + k, nl)
        copy(kvw.at[:, pl.ds(pl.multiple_of(ll * HD, HD), HD)],
             wkv_v.at[pl.ds(pl.multiple_of(l * kvrows, kvrows), kvrows)], S_KVW, g, ll).start()
    each(nl, send_kv)

    def send_h2(k):
        block = q_all.at[h_own, :, c, pl.ds(SPLIT, 4 - SPLIT), par]
        head_copy(block, S_H2, H_H2, h_own, g, lax.rem(l + nl - k, nl)).start()

    def wait_pair(both, one, sem, h):
        @pl.when(h == h_own)
        def _():
            wait_all(one, sem)

        @pl.when(h != h_own)
        def _():
            wait_all(both, sem)

    wait_all(er.at[pl.ds(0, ny - 1), pl.ds(0, 16 * (4 - SPLIT))], recv.at[S_G2])

    def onward(i):
        h = head_at(i)
        wait_pair(q_all.at[h, 0, 0, pl.ds(0, SPLIT)], q_all.at[h, 0, 0, pl.ds(0, SPLIT), 0], by_head.at[H_G1, h], h)

        def send_h1(k):
            gg = lax.rem(y + k, ny) * CORES + c
            head_copy(q_all.at[h, y, c, pl.ds(0, SPLIT)], S_H1, H_H1, h, gg, l).start()
        each(ny, send_h1)

    ahead = min(AHEAD, kvh)
    onward(0)
    each(nl, send_h2)
    each(ahead, onward)

    lane = lax.broadcasted_iota(jnp.int32, (8, 128), 1)
    quarter = (l % 4) * slots
    owners = jnp.full((8, 128), -1, jnp.int32)
    for p in range(slots):
        owners = jnp.where(lane == quarter + p, own_s[p], owners)
    owners = owners.astype(F32)

    which = l // kvh

    def fresh_parts():
        c_kv.wait()
        wait_all(wkv_v.at[pl.ds(0, (nl - 1) * kvrows)], recv.at[S_KVW])
        fpart[...] = jnp.dot(tokens, wkv_v[...], preferred_element_type=F32).reshape(steps, req, HD)
        frs[g] = fpart[:, pl.ds(pl.multiple_of(g * 8, 8), 8), :]

        def send_frs(k):
            gg = lax.rem(g + k, ng)
            copy(fpart.at[:, pl.ds(pl.multiple_of(gg * 8, 8), 8), :], frs.at[g], S_FRS, gg, l).start()
        each(ng, send_frs)

    def fresh_total():
        wait_all(frs.at[pl.ds(0, ng - 1)], recv.at[S_FRS])
        total = frs[0]
        for gg in range(1, ng):
            total = total + frs[gg]
        kvown[...] = total.reshape(steps * 8, HD).astype(BF16)
        for pp in range(2):
            ll = (l % kvh) * 2 + pp

            @pl.when(ll == l)
            def _():
                kv_r[which] = kvown[...]

            for kind in range(2):
                @pl.when((ll != l) & (which == kind))
                def _():
                    copy(kvown, kv_r.at[kind], S_KEY + kind, g, ll).start()

    def to_sibling(i):
        h = head_at(i)
        wait_all(q_all.at[h, pl.ds(0, ny - 1), 0, pl.ds(0, SPLIT)], by_head.at[H_H1, h])
        wait_pair(q_all.at[h, :, 0, pl.ds(SPLIT, 4 - SPLIT)], q_all.at[h, :, 0, pl.ds(SPLIT, 4 - SPLIT), 0],
                  by_head.at[H_H2, h], h)
        head_copy(q_all.at[h, :, c], S_SIB, H_SIB, h, y * CORES + (1 - c), l).start()

    to_sibling(0)
    wait_all(pages_v, local.at[L_PAGES])

    scale = LOG2E / (HD ** 0.5)
    lane16 = lax.broadcasted_iota(jnp.int32, (16, 128), 1)

    def head(i, carry):
        h = head_at(i)
        columns = pl.ds(pl.multiple_of(h * HD, HD), HD)

        @pl.when(i < kvh - ahead)
        def _():
            onward(i + ahead)

        @pl.when(i < kvh - 1)
        def _():
            to_sibling(i + 1)

        wait_all(q_all.at[h, :, 0], by_head.at[H_SIB, h])
        q_head[...] = q_all[h]

        @pl.when(i == (2 if kvh > 2 else 0))
        def _():
            fresh_parts()

        @pl.when(i == (5 if kvh > 5 else 1))
        def _():
            fresh_total()

        def visit(b, state):
            maxima, sums = state
            block = [b * UNROLL + u for u in range(UNROLL)]
            scores = []
            for p in block:
                r = own_s[p]
                scores.append(lax.dot_general(
                    q_head[r // 16, (r // 8) % 2, r % 4, (r // 4) % 2], pages_v[p, 0, :, columns],
                    (((1,), (1,)), ((), ())), preferred_element_type=F32) * scale)
            valid = [lane16 < len_s[p] for p in block]
            scores = [jnp.where(ok, x, NEG) for ok, x in zip(valid, scores)]
            tops = [jnp.max(x, axis=1, keepdims=True) for x in scores]
            weights = [jnp.where(ok, jnp.exp2(x - m), 0.0) for ok, x, m in zip(valid, scores, tops)]
            totals = [jnp.sum(w, axis=1, keepdims=True) for w in weights]
            outs = [
                jnp.dot(w.astype(BF16), pages_v[p, 1, :, columns], preferred_element_type=F32)
                for w, p in zip(weights, block)]
            for p, o, m, t in zip(block, outs, tops, totals):
                slot_o[pl.ds(p, 16, stride=slots), :] = o / jnp.maximum(t, 1e-30)
                here = lane16 == quarter + p
                maxima = jnp.where(here, m, maxima)
                sums = jnp.where(here, t, sums)
            return maxima, sums

        maxima, sums = lax.fori_loop(
            0, slots // UNROLL, visit,
            (jnp.full((16, 128), NEG, F32), jnp.zeros((16, 128), F32)))
        lse = jnp.where(sums > 0.0, maxima + jnp.log(jnp.maximum(sums, 1e-30)) * LOG2E, NEG)
        for half in range(2):
            ll = 2 * h + half
            res[ll, pl.ds(0, 8 * slots)] = slot_o[pl.ds(half * 8 * slots, 8 * slots), :].astype(BF16)
            hi, mid, lo = pieces_of(lse[half * 8:(half + 1) * 8])
            res[ll, pl.ds(8 * slots, 16)] = jnp.concatenate([hi, mid], axis=0).astype(BF16)
            res[ll, pl.ds(8 * slots + 16, 16)] = jnp.concatenate([lo, owners], axis=0).astype(BF16)

            @pl.when(ll != l)
            def _():
                copy(res.at[ll], er.at[l], S_E, g, ll).start()

            @pl.when(ll == l)
            def _():
                er[l] = res[ll]
        return carry

    lax.fori_loop(0, kvh, head, 0)

    for r4 in range(4):
        for pp in range(2):
            qf[(pp * 4 + r4) * 16:(pp * 4 + r4 + 1) * 16] = q_all[h_own, y, c, r4, pp].astype(F32)

    @pl.when(l != h_own)
    def _():
        wait_all(kv_r.at[0], recv.at[S_KEY])

    @pl.when(l != kvh + h_own)
    def _():
        wait_all(kv_r.at[1], recv.at[S_VAL])

    fresh_k = kv_r[0].astype(F32)
    fresh_v = kv_r[1].astype(F32)
    fresh_scores = []
    for i in range(8):
        q_i = qf[pl.ds(par * 8 + i, 8, stride=16), :]
        fresh_scores.append([
            jnp.sum(q_i * fresh_k[t * 8:(t + 1) * 8], axis=1, keepdims=True) * scale
            for t in range(i // 4 + 1)])

    wait_all(er.at[pl.ds(0, nl - 1)], recv.at[S_E])
    request = lax.broadcasted_iota(jnp.int32, (req, 128), 0)
    owned, logs = [], []
    for k in range(nl // 4):
        o = s = None
        for x in range(4 * k, 4 * k + 4):
            tail = er[x, pl.ds(8 * slots, 32)].astype(F32)
            lse = tail[0:8] + tail[8:16] + tail[16:24]
            o = tail[24:32] if o is None else jnp.maximum(o, tail[24:32])
            s = lse if s is None else jnp.maximum(s, lse)
        owned.append(o[0:1].astype(jnp.int32) == request)
        logs.append(s)
    laneq = lax.broadcasted_iota(jnp.int32, (req, 128), 1)
    lse_out = jnp.full((req, 128), NEG, F32)
    for i in range(8):
        masked = [jnp.where(owned[k], logs[k][i:i + 1], NEG) for k in range(nl // 4)]
        m = masked[0]
        for k in range(1, nl // 4):
            m = jnp.maximum(m, masked[k])
        m = jnp.max(m, axis=1, keepdims=True)
        weights = [jnp.where(x > 0.5 * NEG, jnp.exp2(x - m), 0.0) for x in masked]
        t = weights[0]
        for k in range(1, nl // 4):
            t = t + weights[k]
        t = jnp.sum(t, axis=1, keepdims=True)
        weights = jnp.concatenate(weights, axis=1).astype(BF16)
        data = er[:, i * slots:(i + 1) * slots, :].reshape(nl * slots, HD)
        o = jnp.dot(weights, data, preferred_element_type=F32) / jnp.maximum(t, 1e-30)
        ff[:, i * 8:(i + 1) * 8, :] = o.reshape(ng, 8, HD)
        lse = jnp.where(t > 0.0, m + jnp.log(jnp.maximum(t, 1e-30)) * LOG2E, NEG)
        lse_out = jnp.where(laneq == i, lse, lse_out)
    hi, mid, lo = pieces_of(lse_out)
    for k, piece in enumerate((hi, mid, lo, jnp.zeros_like(lo))):
        ff[:, 64 + 8 * k:72 + 8 * k, :] = piece.reshape(ng, 8, 128)
    fb[...] = ff[...].astype(BF16)
    fr[g] = fb[g]

    def send_f(k):
        gg = lax.rem(g + k, ng)
        copy(fb.at[gg], fr.at[g], S_F, gg, l).start()
    each(ng, send_f)

    wait_all(fr.at[pl.ds(0, ng - 1)], recv.at[S_F])
    data = [fr[gg].astype(F32) for gg in range(ng)]
    logs = [x[64:72] + x[72:80] + x[80:88] for x in data]
    for s in range(steps):
        pieces = []
        for j in range(4):
            i = s * 4 + j
            parts = [(logs[gg][:, i:i + 1], data[gg][i * 8:(i + 1) * 8]) for gg in range(ng)]
            parts += [(fresh_scores[i][t], fresh_v[t * 8:(t + 1) * 8]) for t in range(s + 1)]
            m = parts[0][0]
            for score, unused in parts[1:]:
                m = jnp.maximum(m, score)
            total = jnp.zeros((8, 1), F32)
            o = jnp.zeros((8, HD), F32)
            for score, value in parts:
                w = jnp.exp2(score - m)
                total = total + w
                o = o + w * value
            pieces.append(o / total)
        out[s] = jnp.concatenate(pieces, axis=1).astype(BF16)

    wait_all(wkv_v.at[pl.ds(0, (nl - 1) * kvrows)], send.at[S_KVW])
    wait_all(rs.at[pl.ds(0, nch - 1)], send.at[S_RS])
    wait_all(frs.at[pl.ds(0, ng - 1)], send.at[S_FRS])
    wait_all(er.at[pl.ds(0, nl - 1), pl.ds(0, 16 * SPLIT)], send.at[S_G1])
    wait_all(er.at[pl.ds(0, ny - 1), pl.ds(0, 16 * (4 - SPLIT))], send.at[S_G2])
    wait_all(q_all.at[:, pl.ds(0, ny - 1), 0, pl.ds(0, SPLIT)], send.at[S_H1])
    wait_all(er.at[pl.ds(0, nl - 1), pl.ds(0, 16 * ny * (4 - SPLIT))], send.at[S_H2])
    wait_all(q_all.at[:, :, 0], send.at[S_SIB])
    for kind in range(2):
        for pp in range(2):
            @pl.when((which == kind) & ((l % kvh) * 2 + pp != l))
            def _():
                wait_all(kvown, send.at[S_KEY + kind])
    wait_all(er.at[pl.ds(0, nl - 1)], send.at[S_E])
    wait_all(fr.at[pl.ds(0, ng - 1)], send.at[S_F])


def per_device(ng, nl, tokens, query_weight, kv_weight, pages, slot_request, slot_len):
    steps, req, width = tokens.shape
    rows = query_weight.shape[0]
    slots, unused, page, kvwidth = pages.shape
    kvh = kvwidth // HD
    ny = ng // CORES
    hbm = pl.BlockSpec(memory_space=pl.ANY)
    smem = pl.BlockSpec(memory_space=pltpu.SMEM)
    scratch = [
        pltpu.VMEM((steps, req, rows), BF16),
        pltpu.VMEM((rows, 4 * HD), BF16),
        pltpu.VMEM((rows, HD), BF16),
        pltpu.VMEM(pages.shape, BF16),
        pltpu.VMEM((2 * ng, 8, 4 * HD), F32),
        pltpu.VMEM((2 * ng, 8, 4 * HD), F32),
        pltpu.VMEM((steps, req, HD), F32),
        pltpu.VMEM((ng, steps, 8, HD), F32),
        pltpu.VMEM((steps * 8, HD), BF16),
        pltpu.VMEM((2, steps * 8, HD), BF16),
        pltpu.VMEM((kvh, ny, 2, 4, 2, 16, HD), BF16),
        pltpu.VMEM((16 * slots, HD), F32),
        pltpu.VMEM((nl, 8 * slots + 32, HD), BF16),
        pltpu.VMEM((nl, 8 * slots + 32, HD), BF16),
        pltpu.VMEM((ng, 96, HD), F32),
        pltpu.VMEM((ng, 96, HD), BF16),
        pltpu.VMEM((ng, 96, HD), BF16),
        pltpu.VMEM((128, HD), F32),
        pltpu.VMEM((ny, 2, 4, 2, 16, HD), BF16),
        pltpu.SemaphoreType.DMA((12,)),
        pltpu.SemaphoreType.DMA((12,)),
        pltpu.SemaphoreType.DMA((4, kvh)),
        pltpu.SemaphoreType.DMA((4,)),
    ]
    return pl.pallas_call(
        functools.partial(kernel, ng, nl),
        out_shape=jax.ShapeDtypeStruct((steps, req // ng, 4 * HD), BF16),
        in_specs=[hbm, hbm, hbm, hbm, smem, smem],
        out_specs=pl.BlockSpec(memory_space=pltpu.VMEM),
        scratch_shapes=scratch,
        compiler_params=pltpu.CompilerParams(
            collective_id=0, has_side_effects=True, vmem_limit_bytes=62 * 1024 * 1024),
    )(tokens, query_weight, kv_weight, pages, slot_request, slot_len)


def solution(mesh):
    ng, nl = mesh.shape["group"], mesh.shape["lend"]
    return jax.shard_map(
        functools.partial(per_device, ng, nl),
        mesh=mesh,
        in_specs=(
            P(),
            P("group", "lend"),
            P(("group", "lend"), None),
            P(("group", "lend"), None, None, None),
            P(("group", "lend")),
            P(("group", "lend")),
        ),
        out_specs=P(None, "group", "lend"),
        check_vma=False,
    )
```

time: 57.8 us -> 52.3 us (0.905)
  Pallas kernels: 56.3 us -> 50.8 us
    pallas_call x1, Pallas kernels: 56.3 us -> 50.8 us  [per_device(): pl.pallas_call(functools.partial(kernel, ng, nl), out_shape=jax.ShapeDtyp...]
where the time goes in v3:
time: 52.3 us; the launch traced here: 52.1 us
  Pallas kernels  50.8 us (97%)
  local copies, waits for them, and re-layouts  1.32 us (3%)
    pallas_call x1, Pallas kernels, per_device(): pl.pallas_call(functools.partial(kernel, ng, nl), out_shape=jax.ShapeDtyp...  50.8 us
    unnamed x1, local copies, waits for them, and re-layouts  1.32 us

profile of v3, /device:TPU:1, one launch (start us, length us, event | category | flops | bytes accessed | tf_op | source)
XLA Modules:
  0.0 52.1 jit_solution(1232372223118709823)
XLA Ops:
  0.0 50.8 %shard_map.64 = bf16[2,8,512]{2,1,0:T(8,128)(2,1)} custom-call(bf16[2,64,8192]{2,1,0:T(8,128)(2,1)} %tok.1, bf16[1024,512]{1,0:T(8,128)(2,1)} %wq.1, bf16[64,2048]{1,0:T(8,128)(2,1)} %kvw.1, bf16[32,2,128,1024]{3,2,1,0:T(8,128)(2,1)} %pages.1, s32[32]{0:T(128)} %own_s.1, s32[32]{0:T(128)} %len_s.1), custom_call_target="tpu_custom_call" | custom-call | tf_op jit(solution)/shard_map/pallas_call | solution.py:444
  50.8 1.3 %copy.8 = bf16[2,8,512]{2,1,0:T(8,128)(2,1)} copy(bf16[2,8,512]{2,1,0:T(8,128)(2,1)} %shard_map.64) | data formatting | bytes 32768

commit v4 on v3

--- a/solution.py
+++ b/solution.py
@@ -14,7 +14,7 @@
 MESH = pl.DeviceIdType.MESH
 F32 = jnp.float32
 BF16 = jnp.bfloat16
-UNROLL = 16
+UNROLL = 32
 SPLIT = 3
 AHEAD = 8
 
@@ -69,9 +69,9 @@
     def wait_all(ref, sem):
         pltpu.make_async_copy(ref, ref, sem).wait()
 
-    def each(n, body):
+    def each(n, body, far=False):
         def step(k, carry):
-            body(k)
+            body(1 + lax.rem(k + n // 2 - 2, n - 1) if far else k)
             return carry
         lax.fori_loop(1, n, step, 0)
 
@@ -122,7 +122,7 @@
     def send_rs(k):
         idx = lax.rem(mine + k, nch)
         copy(qpart.at[idx], rs.at[mine], S_RS, idx // 2, h_own * 2 + idx % 2).start()
-    each(nch, send_rs)
+    each(nch, send_rs, far=True)
 
     wait_all(rs.at[pl.ds(0, nch - 1)], recv.at[S_RS])
     blocks = []
@@ -139,10 +139,10 @@
     order = jnp.where(fro == source, 1.0, 0.0).astype(BF16)
     chunk = jnp.dot(order, stacked, preferred_element_type=F32).astype(BF16)
     for r4 in range(4):
-        q_all[h_own, y, c, r4, par] = chunk[r4 * 16:(r4 + 1) * 16]
-
-    piece1 = q_all.at[h_own, y, c, pl.ds(0, SPLIT), par]
-    piece2 = q_all.at[h_own, y, c, pl.ds(SPLIT, 4 - SPLIT), par]
+        q_all[h_own, y, c, par, r4] = chunk[r4 * 16:(r4 + 1) * 16]
+
+    piece1 = q_all.at[h_own, y, c, par, pl.ds(0, SPLIT)]
+    piece2 = q_all.at[h_own, y, c, par, pl.ds(SPLIT, 4 - SPLIT)]
 
     def send_g2(k):
         copy(piece2, piece2, S_G2, lax.rem(y + k, ny) * CORES + c, l).start()
@@ -150,7 +150,36 @@
 
     def send_g1(k):
         head_copy(piece1, S_G1, H_G1, h_own, g, lax.rem(l + nl - k, nl)).start()
-    each(nl, send_g1)
+    each(nl, send_g1, far=True)
+
+    def send_h2(k):
+        block = q_all.at[h_own, :, c, par, pl.ds(SPLIT, 4 - SPLIT)]
+        head_copy(block, S_H2, H_H2, h_own, g, lax.rem(l + nl - k, nl)).start()
+
+    def wait_pair(both, one, sem, h):
+        @pl.when(h == h_own)
+        def _():
+            wait_all(one, sem)
+
+        @pl.when(h != h_own)
+        def _():
+            wait_all(both, sem)
+
+    wait_all(er.at[pl.ds(0, ny - 1), pl.ds(0, 16 * (4 - SPLIT))], recv.at[S_G2])
+
+    def onward(i):
+        h = head_at(i)
+        wait_pair(q_all.at[h, 0, 0, :, pl.ds(0, SPLIT)], q_all.at[h, 0, 0, 0, pl.ds(0, SPLIT)], by_head.at[H_G1, h], h)
+
+        def send_h1(k):
+            gg = lax.rem(y + k, ny) * CORES + c
+            head_copy(q_all.at[h, y, c, :, pl.ds(0, SPLIT)], S_H1, H_H1, h, gg, l).start()
+        each(ny, send_h1)
+
+    ahead = min(AHEAD, kvh)
+    onward(0)
+    each(nl, send_h2)
+    each(ahead, onward)
 
     def send_kv(k):
         ll = lax.rem(l + k, nl)
@@ -158,40 +187,10 @@
              wkv_v.at[pl.ds(pl.multiple_of(l * kvrows, kvrows), kvrows)], S_KVW, g, ll).start()
     each(nl, send_kv)
 
-    def send_h2(k):
-        block = q_all.at[h_own, :, c, pl.ds(SPLIT, 4 - SPLIT), par]
-        head_copy(block, S_H2, H_H2, h_own, g, lax.rem(l + nl - k, nl)).start()
-
-    def wait_pair(both, one, sem, h):
-        @pl.when(h == h_own)
-        def _():
-            wait_all(one, sem)
-
-        @pl.when(h != h_own)
-        def _():
-            wait_all(both, sem)
-
-    wait_all(er.at[pl.ds(0, ny - 1), pl.ds(0, 16 * (4 - SPLIT))], recv.at[S_G2])
-
-    def onward(i):
-        h = head_at(i)
-        wait_pair(q_all.at[h, 0, 0, pl.ds(0, SPLIT)], q_all.at[h, 0, 0, pl.ds(0, SPLIT), 0], by_head.at[H_G1, h], h)
-
-        def send_h1(k):
-            gg = lax.rem(y + k, ny) * CORES + c
-            head_copy(q_all.at[h, y, c, pl.ds(0, SPLIT)], S_H1, H_H1, h, gg, l).start()
-        each(ny, send_h1)
-
-    ahead = min(AHEAD, kvh)
-    onward(0)
-    each(nl, send_h2)
-    each(ahead, onward)
-
     lane = lax.broadcasted_iota(jnp.int32, (8, 128), 1)
-    quarter = (l % 4) * slots
     owners = jnp.full((8, 128), -1, jnp.int32)
     for p in range(slots):
-        owners = jnp.where(lane == quarter + p, own_s[p], owners)
+        owners = jnp.where(lane == p, own_s[p], owners)
     owners = owners.astype(F32)
 
     which = l // kvh
@@ -227,8 +226,8 @@
 
     def to_sibling(i):
         h = head_at(i)
-        wait_all(q_all.at[h, pl.ds(0, ny - 1), 0, pl.ds(0, SPLIT)], by_head.at[H_H1, h])
-        wait_pair(q_all.at[h, :, 0, pl.ds(SPLIT, 4 - SPLIT)], q_all.at[h, :, 0, pl.ds(SPLIT, 4 - SPLIT), 0],
+        wait_all(q_all.at[h, pl.ds(0, ny - 1), 0, :, pl.ds(0, SPLIT)], by_head.at[H_H1, h])
+        wait_pair(q_all.at[h, :, 0, :, pl.ds(SPLIT, 4 - SPLIT)], q_all.at[h, :, 0, 0, pl.ds(SPLIT, 4 - SPLIT)],
                   by_head.at[H_H2, h], h)
         head_copy(q_all.at[h, :, c], S_SIB, H_SIB, h, y * CORES + (1 - c), l).start()
 
@@ -268,7 +267,7 @@
             for p in block:
                 r = own_s[p]
                 scores.append(lax.dot_general(
-                    q_head[r // 16, (r // 8) % 2, r % 4, (r // 4) % 2], pages_v[p, 0, :, columns],
+                    q_head[r // 16, (r // 8) % 2, (r // 4) % 2, r % 4], pages_v[p, 0, :, columns],
                     (((1,), (1,)), ((), ())), preferred_element_type=F32) * scale)
             valid = [lane16 < len_s[p] for p in block]
             scores = [jnp.where(ok, x, NEG) for ok, x in zip(valid, scores)]
@@ -280,7 +279,7 @@
                 for w, p in zip(weights, block)]
             for p, o, m, t in zip(block, outs, tops, totals):
                 slot_o[pl.ds(p, 16, stride=slots), :] = o / jnp.maximum(t, 1e-30)
-                here = lane16 == quarter + p
+                here = lane16 == p
                 maxima = jnp.where(here, m, maxima)
                 sums = jnp.where(here, t, sums)
             return maxima, sums
@@ -293,8 +292,10 @@
             ll = 2 * h + half
             res[ll, pl.ds(0, 8 * slots)] = slot_o[pl.ds(half * 8 * slots, 8 * slots), :].astype(BF16)
             hi, mid, lo = pieces_of(lse[half * 8:(half + 1) * 8])
-            res[ll, pl.ds(8 * slots, 16)] = jnp.concatenate([hi, mid], axis=0).astype(BF16)
-            res[ll, pl.ds(8 * slots + 16, 16)] = jnp.concatenate([lo, owners], axis=0).astype(BF16)
+            tail = hi
+            for k, piece in enumerate((mid, lo, owners), 1):
+                tail = jnp.where(lane < k * slots, tail, pltpu.roll(piece, k * slots, 1))
+            res[ll, pl.ds(8 * slots, 16)] = jnp.concatenate([tail, tail], axis=0).astype(BF16)
 
             @pl.when(ll != l)
             def _():
@@ -309,7 +310,7 @@
 
     for r4 in range(4):
         for pp in range(2):
-            qf[(pp * 4 + r4) * 16:(pp * 4 + r4 + 1) * 16] = q_all[h_own, y, c, r4, pp].astype(F32)
+            qf[(pp * 4 + r4) * 16:(pp * 4 + r4 + 1) * 16] = q_all[h_own, y, c, pp, r4].astype(F32)
 
     @pl.when(l != h_own)
     def _():
@@ -333,11 +334,13 @@
     owned, logs = [], []
     for k in range(nl // 4):
         o = s = None
-        for x in range(4 * k, 4 * k + 4):
-            tail = er[x, pl.ds(8 * slots, 32)].astype(F32)
-            lse = tail[0:8] + tail[8:16] + tail[16:24]
-            o = tail[24:32] if o is None else jnp.maximum(o, tail[24:32])
-            s = lse if s is None else jnp.maximum(s, lse)
+        for q in range(4):
+            tail = er[4 * k + q, pl.ds(8 * slots, 16)].astype(F32)[0:8]
+            lse = tail + pltpu.roll(tail, 3 * slots, 1) + pltpu.roll(tail, 2 * slots, 1)
+            owner = pltpu.roll(tail, (q + 1) * slots % 128, 1) if q < 3 else tail
+            lse = pltpu.roll(lse, q * slots, 1) if q else lse
+            o = owner if o is None else jnp.where(lane < q * slots, o, owner)
+            s = lse if s is None else jnp.where(lane < q * slots, s, lse)
         owned.append(o[0:1].astype(jnp.int32) == request)
         logs.append(s)
     laneq = lax.broadcasted_iota(jnp.int32, (req, 128), 1)
@@ -368,7 +371,7 @@
     def send_f(k):
         gg = lax.rem(g + k, ng)
         copy(fb.at[gg], fr.at[g], S_F, gg, l).start()
-    each(ng, send_f)
+    each(ng, send_f, far=True)
 
     wait_all(fr.at[pl.ds(0, ng - 1)], recv.at[S_F])
     data = [fr[gg].astype(F32) for gg in range(ng)]
@@ -396,7 +399,7 @@
     wait_all(frs.at[pl.ds(0, ng - 1)], send.at[S_FRS])
     wait_all(er.at[pl.ds(0, nl - 1), pl.ds(0, 16 * SPLIT)], send.at[S_G1])
     wait_all(er.at[pl.ds(0, ny - 1), pl.ds(0, 16 * (4 - SPLIT))], send.at[S_G2])
-    wait_all(q_all.at[:, pl.ds(0, ny - 1), 0, pl.ds(0, SPLIT)], send.at[S_H1])
+    wait_all(q_all.at[:, pl.ds(0, ny - 1), 0, :, pl.ds(0, SPLIT)], send.at[S_H1])
     wait_all(er.at[pl.ds(0, nl - 1), pl.ds(0, 16 * ny * (4 - SPLIT))], send.at[S_H2])
     wait_all(q_all.at[:, :, 0], send.at[S_SIB])
     for kind in range(2):
@@ -427,15 +430,15 @@
         pltpu.VMEM((ng, steps, 8, HD), F32),
         pltpu.VMEM((steps * 8, HD), BF16),
         pltpu.VMEM((2, steps * 8, HD), BF16),
-        pltpu.VMEM((kvh, ny, 2, 4, 2, 16, HD), BF16),
+        pltpu.VMEM((kvh, ny, 2, 2, 4, 16, HD), BF16),
         pltpu.VMEM((16 * slots, HD), F32),
-        pltpu.VMEM((nl, 8 * slots + 32, HD), BF16),
-        pltpu.VMEM((nl, 8 * slots + 32, HD), BF16),
+        pltpu.VMEM((nl, 8 * slots + 16, HD), BF16),
+        pltpu.VMEM((nl, 8 * slots + 16, HD), BF16),
         pltpu.VMEM((ng, 96, HD), F32),
         pltpu.VMEM((ng, 96, HD), BF16),
         pltpu.VMEM((ng, 96, HD), BF16),
         pltpu.VMEM((128, HD), F32),
-        pltpu.VMEM((ny, 2, 4, 2, 16, HD), BF16),
+        pltpu.VMEM((ny, 2, 2, 4, 16, HD), BF16),
         pltpu.SemaphoreType.DMA((12,)),
         pltpu.SemaphoreType.DMA((12,)),
         pltpu.SemaphoreType.DMA((4, kvh)),

time: 52.3 us -> 51.6 us (0.987)
  Pallas kernels: 50.8 us -> 50 us
    pallas_call x1, Pallas kernels: 50.8 us -> 50 us  [per_device(): pl.pallas_call(functools.partial(kernel, ng, nl), out_shape=jax.ShapeDtyp...]
where the time goes in v4:
time: 51.6 us; the launch traced here: 51.4 us
  Pallas kernels  50 us (97%)
  local copies, waits for them, and re-layouts  1.32 us (3%)
    pallas_call x1, Pallas kernels, per_device(): pl.pallas_call(functools.partial(kernel, ng, nl), out_shape=jax.ShapeDtyp...  50 us
    unnamed x1, local copies, waits for them, and re-layouts  1.32 us

profile of v4, /device:TPU:1, one launch (start us, length us, event | category | flops | bytes accessed | tf_op | source)
XLA Modules:
  0.0 51.4 jit_solution(17592470621629958930)
XLA Ops:
  0.0 50.0 %shard_map.64 = bf16[2,8,512]{2,1,0:T(8,128)(2,1)} custom-call(bf16[2,64,8192]{2,1,0:T(8,128)(2,1)} %tok.1, bf16[1024,512]{1,0:T(8,128)(2,1)} %wq.1, bf16[64,2048]{1,0:T(8,128)(2,1)} %kvw.1, bf16[32,2,128,1024]{3,2,1,0:T(8,128)(2,1)} %pages.1, s32[32]{0:T(128)} %own_s.1, s32[32]{0:T(128)} %len_s.1), custom_call_target="tpu_custom_call" | custom-call | tf_op jit(solution)/shard_map/pallas_call | solution.py:447
  50.0 1.3 %copy.8 = bf16[2,8,512]{2,1,0:T(8,128)(2,1)} copy(bf16[2,8,512]{2,1,0:T(8,128)(2,1)} %shard_map.64) | data formatting | bytes 32768

commit v5 on v4

--- a/solution.py
+++ b/solution.py
@@ -146,7 +146,7 @@
 
     def send_g2(k):
         copy(piece2, piece2, S_G2, lax.rem(y + k, ny) * CORES + c, l).start()
-    each(ny, send_g2)
+    each(ny, send_g2, far=True)
 
     def send_g1(k):
         head_copy(piece1, S_G1, H_G1, h_own, g, lax.rem(l + nl - k, nl)).start()
@@ -174,7 +174,7 @@
         def send_h1(k):
             gg = lax.rem(y + k, ny) * CORES + c
             head_copy(q_all.at[h, y, c, :, pl.ds(0, SPLIT)], S_H1, H_H1, h, gg, l).start()
-        each(ny, send_h1)
+        each(ny, send_h1, far=True)
 
     ahead = min(AHEAD, kvh)
     onward(0)
@@ -252,11 +252,11 @@
         wait_all(q_all.at[h, :, 0], by_head.at[H_SIB, h])
         q_head[...] = q_all[h]
 
-        @pl.when(i == (2 if kvh > 2 else 0))
+        @pl.when(i == (3 if kvh > 2 else 0))
         def _():
             fresh_parts()
 
-        @pl.when(i == (5 if kvh > 5 else 1))
+        @pl.when(i == (6 if kvh > 5 else 1))
         def _():
             fresh_total()
 

time: 51.6 us -> 51.6 us (level)
  no operation moved by 1% of the time
where the time goes in v5:
time: 51.6 us; the launch traced here: 51.4 us
  Pallas kernels  50.1 us (97%)
  local copies, waits for them, and re-layouts  1.32 us (3%)
    pallas_call x1, Pallas kernels, per_device(): pl.pallas_call(functools.partial(kernel, ng, nl), out_shape=jax.ShapeDtyp...  50.1 us
    unnamed x1, local copies, waits for them, and re-layouts  1.32 us

profile of v5, /device:TPU:1, one launch (start us, length us, event | category | flops | bytes accessed | tf_op | source)
XLA Modules:
  0.0 51.4 jit_solution(16587601693727081987)
XLA Ops:
  0.0 50.1 %shard_map.64 = bf16[2,8,512]{2,1,0:T(8,128)(2,1)} custom-call(bf16[2,64,8192]{2,1,0:T(8,128)(2,1)} %tok.1, bf16[1024,512]{1,0:T(8,128)(2,1)} %wq.1, bf16[64,2048]{1,0:T(8,128)(2,1)} %kvw.1, bf16[32,2,128,1024]{3,2,1,0:T(8,128)(2,1)} %pages.1, s32[32]{0:T(128)} %own_s.1, s32[32]{0:T(128)} %len_s.1), custom_call_target="tpu_custom_call" | custom-call | tf_op jit(solution)/shard_map/pallas_call | solution.py:447
  50.1 1.3 %copy.8 = bf16[2,8,512]{2,1,0:T(8,128)(2,1)} copy(bf16[2,8,512]{2,1,0:T(8,128)(2,1)} %shard_map.64) | data formatting | bytes 32768
